TPU v7x, 512 devices: a whole 4x8x8 slice. The times are simulated.
512 devices in a mesh: dp: 32 (over z_hi, x, core), fsdp: 16 (over y, z_lo).
Axes of the slice: x: 4, y: 8, z: 8 (z_hi: 4, z_lo: 2; z = z_hi * 2 + z_lo), core: 2. Of those that a mesh axis runs over, the one named last changes fastest.
Arguments:
- tokens: bfloat16 [4096, 8192], P('dp', 'fsdp'), may hold values from -6 to 6
- cotangent: bfloat16 [4096, 4096], P('dp', 'fsdp'), may hold values from -6 to 6
- blocks: bfloat16 [1024, 128, 128], P('fsdp'), may hold values from -0.125 to 0.125
- slot_block: int32 [1024], P('fsdp'), may hold values from 0 to 2047, as said below
- shard_count: int32 [16], P('fsdp'), may hold values from 1 to 64, 512 in all
Outputs:
- projected: bfloat16 [4096, 4096], P('dp', 'fsdp')
- input_grad: bfloat16 [4096, 8192], P('dp', 'fsdp')
- block_grad: bfloat16 [1024, 128, 128], P('fsdp')
Inputs may be any that keep to these rules, and one draw needn't show every extreme that they name: The first shard_count[q] slots of group q are its live slots; the entries sum to 512. `slot_block`: all entries are distinct; the block of slot s has its column c in the band of group s // 64, that is c * 16 // 32 == s // 64.
All inputs are finite; a program needn't handle non-finite values.
Results may differ from a plain program's by a relative error of at most 0.001.
Values may be sent and summed in bfloat16 or wider, within the bound.
A program may use at most 128 MiB of HBM per device.

v0:
```python
import jax
import jax.numpy as jnp
from jax import lax
from jax.sharding import Mesh
from jax.sharding import PartitionSpec as P

DOUT = 4096
BLK = 128
DP = ("dp_0", "dp_1", "dp_2")
FSDP = ("fsdp_0", "fsdp_1")


def cut_along(value, dim, length):
    before, after = (value.shape[:dim], value.shape[dim + 1 :])
    return jnp.moveaxis(value.reshape(*before, length, -1, *after), dim, 0)


def sent_and_summed(value, axis, dim):
    length = lax.axis_size(axis)
    pieces = lax.all_to_all(cut_along(value, dim, length), axis, 0, 0, tiled=True)
    return jnp.sum(pieces, axis=0)


def sum_by_axis(value, axes, dim):
    far, near = axes
    own = sent_and_summed(cut_along(value, dim, lax.axis_size(far)), near, dim + 1)
    return jnp.sum(lax.all_to_all(own, far, 0, 0, tiled=True), axis=0)


def padded_to(lines, length):
    spare = -len(lines) % length
    return jnp.pad(lines, [(0, spare)] + [(0, 0)] * (lines.ndim - 1))


def copy_for_each(value, axis):
    copies = jnp.broadcast_to(value, (lax.axis_size(axis), *value.shape))
    return lax.all_to_all(copies, axis, split_axis=0, concat_axis=0, tiled=True)


def laid_out(pieces, dim):
    lengths = list(pieces.shape[1:])
    lengths[dim] *= pieces.shape[0]
    return jnp.moveaxis(pieces, 0, dim).reshape(lengths)


def gathered_by_axis(value, axes, dim):
    far, near = axes
    first = copy_for_each(value, far)
    pieces = jnp.swapaxes(copy_for_each(first, near), 0, 1)
    return laid_out(pieces.reshape(-1, *value.shape), dim)


def total_of(value, axes):
    lines = value.reshape(-1, value.shape[-1])
    own = sum_by_axis(padded_to(lines, lax.axis_size(axes[0]) * lax.axis_size(axes[1])), axes, 0)
    whole = gathered_by_axis(own, axes, 0)
    return whole[: len(lines)].reshape(value.shape)


def gather_directly(value, axis, dim):
    pieces = copy_for_each(value, axis)
    return laid_out(pieces, dim)


def sum_by_axis_2(value, axes, dim):
    if not axes:
        return value
    nearer = lax.psum_scatter(value, axes[0], scatter_dimension=dim, tiled=True)
    return sum_by_axis_2(nearer, axes[1:], dim)


def slot_cells(slot_ids, low_pos, high_pos, per_band):
    n_out_all = DOUT // BLK
    position = jnp.arange(slot_ids.shape[0], dtype=jnp.int32)
    live_mask = (position >= low_pos) & (position < high_pos)
    row_ids = slot_ids // n_out_all
    col_local = slot_ids % n_out_all % per_band
    return (row_ids * per_band + col_local, live_mask)


def band_matrix(weights, slot_ids, low_pos, high_pos, n_in, per_band):
    cells, live_mask = slot_cells(slot_ids, low_pos, high_pos, per_band)
    slot_total = weights.shape[0]
    picker = (cells[:, None] == jnp.arange(n_in * per_band, dtype=jnp.int32)[None, :]) & live_mask[
        :, None
    ]
    picker = picker.astype(jnp.bfloat16)
    flat = lax.dot_general(
        picker,
        weights.reshape(slot_total, BLK * BLK),
        (((0,), (0,)), ((), ())),
        preferred_element_type=jnp.float32,
    )
    dense = flat.astype(jnp.bfloat16).reshape(n_in, per_band, BLK, BLK)
    return dense.transpose(0, 2, 1, 3).reshape(n_in * BLK, per_band * BLK)


def block_grads(x_full, g_full, slot_ids, low_pos, high_pos, n_in, per_band):
    cells, live_mask = slot_cells(slot_ids, low_pos, high_pos, per_band)
    outer = lax.dot_general(
        x_full, g_full, (((0,), (0,)), ((), ())), preferred_element_type=jnp.float32
    )
    tiles = (
        outer.reshape(n_in, BLK, per_band, BLK)
        .transpose(0, 2, 1, 3)
        .reshape(n_in * per_band, BLK, BLK)
    )
    picked = jnp.take(tiles, cells, axis=0)
    return jnp.where(live_mask[:, None, None], picked, jnp.zeros_like(picked))


def apply_band(x_full, band):
    return jnp.dot(x_full, band, preferred_element_type=jnp.float32)


def apply_transposed(g_full, band):
    return lax.dot_general(
        g_full, band, (((1,), (1,)), ((), ())), preferred_element_type=jnp.float32
    )


def sum_over_data(dw_acc):
    return total_of(dw_acc, (("dp_0", "dp_1"), "dp_2")).astype(jnp.bfloat16)


def per_device(tokens, cotangent, blocks, slot_block, shard_count):
    x_full = gather_directly(tokens, FSDP, 1)
    n_in = x_full.shape[1] // BLK
    per_band = cotangent.shape[1] // BLK
    own_count = shard_count[0]
    band = band_matrix(blocks, slot_block, 0, own_count, n_in, per_band)
    y_total = apply_band(x_full, band)
    dx_acc = apply_transposed(cotangent, band)
    dw_acc = block_grads(x_full, cotangent, slot_block, 0, own_count, n_in, per_band)
    dx_local = sum_by_axis_2(dx_acc, FSDP, 1)
    dw_total = sum_over_data(dw_acc)
    return (y_total.astype(jnp.bfloat16), dx_local.astype(jnp.bfloat16), dw_total)


def solution(mesh):
    split = Mesh(mesh.devices.reshape(4, 4, 2, 8, 2), ("dp_0", "dp_1", "dp_2", "fsdp_0", "fsdp_1"))
    return jax.shard_map(
        per_device,
        mesh=split,
        in_specs=(P(DP, FSDP), P(DP, FSDP), P(FSDP, None, None), P(FSDP), P(FSDP)),
        out_specs=(P(DP, FSDP), P(DP, FSDP), P(FSDP, None, None)),
        check_vma=False,
    )
```

profile of v0, /device:TPU:1, one launch (start us, length us, event | category | flops | bytes accessed | tf_op | source)
XLA Modules:
  0.0 218.6 jit_solution(2105139341024351463)
XLA Ops:
  7.2 0.0 copy-start.1
  7.2 1.0 copy.37
  8.2 1.7 broadcast_in_dim.46
  9.9 9.6 %all-to-all-start = ((bf16[16,128,512]{1,2,0:T(8,128)(2,1)}), bf16[16,128,512]{1,2,0:T(8,128)(2,1)S(1)}, u32[]{:S(2)}, u32[]{:S(2)}) async-start(bf16[16,128,512]{1,2,0:T(8,128)(2,1)} %broadcast_in_dim.46), calls=%async_computation | async-start | bytes 4194304 | tf_op jit(solution)/shard_map/all_to_all | solution.py:37
  19.5 0.0 reduce-scatter.3.cloned.1.call-start
  20.2 0.0 copy-done.1
  20.2 3.3 %fusion.5 = bf16[16,8,128,128]{3,1,2,0:T(8,128)(2,1)S(1)} fusion(bf16[8,8,128,128]{3,2,1,0:T(8,128)(2,1)} %bitcast.68, s32[64]{0:T(128)S(1)} %get-tuple-element.19, pred[64]{0:T(512)(128)(4,1)S(1)} %get-tuple-element.20), kind=kOutput, calls=%fused_computation.10 | convolution fusion | flops 270548992 | bytes 6291776 | tf_op jit(solution)/shard_map/dot_general | solution.py:88
  23.5 3.2 %copy.49 = bf16[16,8,128,128]{3,2,1,0:T(8,128)(2,1)} copy(bf16[16,8,128,128]{3,1,2,0:T(8,128)(2,1)S(1)} %fusion.5) | data formatting | bytes 8388608
  26.7 0.0 copy-start
  26.7 6.7 %copy.36 = bf16[64,2,128,128]{2,0,3,1:T(8,128)(2,1)} copy(bf16[64,2,128,128]{3,2,1,0:T(8,128)(2,1)} %bitcast.65) | data formatting | bytes 8388608 | tf_op jit(solution)/shard_map/reshape | solution.py:94
  33.4 0.0 copy-done
  33.4 9.1 %convolution_bitcast_fusion = f32[128,8192]{0,1:T(8,128)} fusion(bf16[128,256]{1,0:T(8,128)(2,1)S(1)} %copy-done, bf16[32,8,64,128]{3,2,1,0:T(8,128)(2,1)} %bitcast.61), kind=kOutput, calls=%fused_computation.2 | convolution fusion | flops 536870912 | bytes 8454144 | tf_op jit(solution)/shard_map/dot_general | solution.py:117
  42.5 0.0 reduce-scatter.3.cloned.1.call-update
  42.5 0.1 copy.47
  42.7 0.1 broadcast_in_dim.50
  42.8 0.1 broadcast_in_dim.51
  43.0 0.1 broadcast_in_dim.47
  43.2 25.5 %all-to-all-done = bf16[16,128,512]{1,2,0:T(8,128)(2,1)S(1)} async-done(((bf16[16,128,512]{1,2,0:T(8,128)(2,1)}), bf16[16,128,512]{1,2,0:T(8,128)(2,1)S(1)}, u32[]{:S(2)}, u32[]{:S(2)}) %all-to-all-start) | async-done | bytes 2097184 | tf_op jit(solution)/shard_map/all_to_all | solution.py:37
  68.7 4.5 %fusion.21 = f32[64,128,2,128]{3,1,2,0:T(8,128)} fusion(bf16[64,128,128,1]{2,1,3,0:T(8,128)(2,1)S(1)} %bitcast.66, bf16[2,128,128,1]{2,1,0,3:T(8,128)(2,1)S(1)} %bitcast.71), kind=kOutput, calls=%fused_computation.34 | convolution fusion | flops 536870912 | bytes 10551296 | tf_op jit(solution)/shard_map/dot_general | solution.py:100
  73.1 6.2 %gather_fusion = f32[64,128,128]{2,1,0:T(8,128)} fusion(f32[128,128,128]{2,1,0:T(8,128)} %bitcast.63, s32[1024]{0:T(1024)S(1)} %pad_clamp_fusion), kind=kCustom, calls=%fused_computation | custom fusion | bytes 8388864 | tf_op jit(solution)/shard_map/jit(_take)/gather | solution.py:108
  79.4 6.0 %select_bitcast_fusion = f32[2,16,256,128]{3,2,0,1:T(8,128)S(1)} fusion(f32[16,2,256,128]{3,2,1,0:T(8,128)} %bitcast.64, pred[16,2,256]{2,1,0:T(4,128)(4,1)S(1)} %copy.40, pred[16,2,256]{2,1,0:T(4,128)(4,1)S(1)} %copy.38), kind=kLoop, calls=%fused_computation.7 | loop fusion | flops 2097152 | bytes 8404992 | tf_op jit(solution)/shard_map/transpose | solution.py:15
  85.4 0.4 copy.42
  85.9 11.5 %all_to_all.25 = f32[2,16,256,128]{3,2,1,0:T(8,128)} all-to-all(f32[2,16,256,128]{3,2,1,0:T(8,128)S(1)} %copy.42), channel_id=1, replica_groups=mesh['dp_0'=4,'dp_1'=4,'dp_2'=2,'fsdp_0'=8,'fsdp_1'=2] {'dp_2'}, dimensions={0} | all-to-all | bytes 8388608 | tf_op jit(solution)/shard_map/all_to_all | solution.py:20
  97.4 4.1 %reduce_sum.18 = f32[16,256,128]{2,1,0:T(8,128)} reduce(f32[2,16,256,128]{3,2,1,0:T(8,128)} %all_to_all.25, f32[]{:T(128)} %constant.70.clone.1), dimensions={0}, to_apply=%region_2.3 | reduce | flops 524288 | bytes 6291460 | tf_op jit(solution)/shard_map/reduce_sum | solution.py:21
  101.4 65.2 %all_to_all.26 = f32[16,256,128]{2,1,0:T(8,128)} all-to-all(f32[16,256,128]{2,1,0:T(8,128)} %reduce_sum.18), channel_id=1, replica_groups=mesh['dp_0'=4,'dp_1'=4,'dp_2'=2,'fsdp_0'=8,'fsdp_1'=2] {'dp_0','dp_1'}, dimensions={0} | all-to-all | bytes 4194304 | tf_op jit(solution)/shard_map/all_to_all | solution.py:27
  166.6 1.7 reduce_sum.19
  168.3 1.2 broadcast_in_dim.57
  169.4 5.0 %all-to-all-start.3 = ((bf16[16,256,128]{2,1,0:T(8,128)(2,1)}), bf16[16,256,128]{2,1,0:T(8,128)(2,1)S(1)}, u32[]{:S(2)}, u32[]{:S(2)}) async-start(bf16[16,256,128]{2,1,0:T(8,128)(2,1)} %broadcast_in_dim.57), calls=%async_computation.5 | async-start | bytes 2097152 | tf_op jit(solution)/shard_map/all_to_all | solution.py:37
  174.5 0.0 reduce-scatter.5.cloned.1.call-start
  174.5 0.0 reduce-scatter.3.cloned.1.call-done
  174.5 0.7 reduce-scatter.5.cloned.1.call-update
  175.2 4.8 %fusion.11 = bf16[128,256]{0,1:T(8,128)(2,1)S(1)} fusion(bf16[128,8192]{0,1:T(8,128)(2,1)S(1)} %bitcast.67, bf16[32,8,64,128]{3,2,1,0:T(8,128)(2,1)} %bitcast.62), kind=kOutput, calls=%fused_computation.14 | convolution fusion | flops 536903680 | bytes 6356992 | tf_op jit(solution)/shard_map/dot_general | solution.py:113
  180.0 0.7 copy.44
  180.8 21.6 %reduce-scatter.5.cloned.1.call-done = f32[128,512]{0,1:T(8,128)} async-done(((f32[128,1024]{0,1:T(8,128)}), f32[128,512]{0,1:T(8,128)}) %reduce-scatter.5.cloned.1.call-update) | async-done | bytes 262160 | tf_op jit(solution)/shard_map/reduce_scatter | solution.py:68
  202.3 1.0 convert_element_type.25
  203.3 0.8 copy.45
  204.1 0.0 all-to-all-done.3
  204.1 0.5 broadcast_in_dim.58
  204.5 5.7 %all_to_all.27 = bf16[2,16,256,128]{3,2,1,0:T(8,128)(2,1)S(1)} all-to-all(bf16[2,16,256,128]{3,2,1,0:T(8,128)(2,1)S(1)} %broadcast_in_dim.58), channel_id=1, replica_groups=mesh['dp_0'=4,'dp_1'=4,'dp_2'=2,'fsdp_0'=8,'fsdp_1'=2] {'dp_2'}, dimensions={0} | all-to-all | bytes 4194304 | tf_op jit(solution)/shard_map/all_to_all | solution.py:37
  210.3 1.5 copy.68
  (9 shorter events, 0.2 us)
Async XLA Ops:
  7.2 13.0 %copy-start.1 = (s32[64]{0:T(128)S(1)}, s32[64]{0:T(128)}, u32[]{:S(2)}) copy-start(s32[64]{0:T(128)} %param.8) | copy-start | bytes 772
  9.9 58.7 %all-to-all-start = ((bf16[16,128,512]{1,2,0:T(8,128)(2,1)}), bf16[16,128,512]{1,2,0:T(8,128)(2,1)S(1)}, u32[]{:S(2)}, u32[]{:S(2)}) async-start(bf16[16,128,512]{1,2,0:T(8,128)(2,1)} %broadcast_in_dim.46), calls=%async_computation | async-start | bytes 4194304 | tf_op jit(solution)/shard_map/all_to_all | solution.py:37
  19.5 155.0 %reduce-scatter.3.cloned.1.call-start = ((), (), s32[]{:S(2)}) async-start(), calls=%async_computation.7 | async-start | bytes 4718592 | tf_op jit(solution)/shard_map/reduce_scatter | solution.py:68
  26.7 6.7 %copy-start = (bf16[128,256]{1,0:T(8,128)(2,1)S(1)}, bf16[128,256]{1,0:T(8,128)(2,1)}, u32[]{:S(2)}) copy-start(bf16[128,256]{1,0:T(8,128)(2,1)} %param.6) | copy-start | bytes 196612
  169.4 34.6 %all-to-all-start.3 = ((bf16[16,256,128]{2,1,0:T(8,128)(2,1)}), bf16[16,256,128]{2,1,0:T(8,128)(2,1)S(1)}, u32[]{:S(2)}, u32[]{:S(2)}) async-start(bf16[16,256,128]{2,1,0:T(8,128)(2,1)} %broadcast_in_dim.57), calls=%async_computation.5 | async-start | bytes 2097152 | tf_op jit(solution)/shard_map/all_to_all | solution.py:37
  174.5 27.9 %reduce-scatter.5.cloned.1.call-start = ((), (), s32[]{:S(2)}) async-start(), calls=%async_computation.8 | async-start | bytes 786432 | tf_op jit(solution)/shard_map/reduce_scatter | solution.py:68
Sparse Core Ops, SparseCore 0:
  42.7 66.1 reduce-scatter.2
  178.1 24.1 reduce-scatter.4
where the time goes:
time: 220 us; the launch traced here: 219 us
  blocking collectives  82.4 us (37%)
  waiting for transfers between devices  47.8 us (22%)
  local copies, waits for them, and re-layouts  24.4 us (11%)
  matrix products  21.7 us (10%)
  between operations  14.9 us (7%)
  starting transfers between devices  14.7 us (7%)
  other arithmetic  12.8 us (6%)
    all_to_all x1, blocking collectives, sum_by_axis(): return jnp.sum(lax.all_to_all(own, far, 0, 0, tiled=True), axis=0)  65.2 us
    all_to_all x2, waiting for transfers between devices, copy_for_each(): return lax.all_to_all(copies, axis, split_axis=0, concat_axis=0, tiled=True)  25.5 us
    reduce_scatter x2, waiting for transfers between devices, sum_by_axis_2(): nearer = lax.psum_scatter(value, axes[0], scatter_dimension=dim, tiled=True)  21.6 us
    all_to_all x2, starting transfers between devices, copy_for_each(): return lax.all_to_all(copies, axis, split_axis=0, concat_axis=0, tiled=True)  14.6 us
    all_to_all x1, blocking collectives, sent_and_summed(): lax.all_to_all(cut_along(value, dim, length), axis, 0, 0, tiled=True)  11.5 us
    dot_general x1, matrix products, apply_transposed(): lax.dot_general(g_full, band, (((1,), (1,)), ((), ())), preferred_element...  9.14 us
    reshape x1, local copies, waits for them, and re-layouts, band_matrix(): dense = flat.astype(jnp.bfloat16).reshape(n_in, per_band, BLK, BLK)  6.66 us
    gather x1, local copies, waits for them, and re-layouts, block_grads(): picked = jnp.take(tiles, cells, axis=0)  6.23 us
  transfers between devices with their start and end apart: 4, of which 2 were waited for; matrix products, arithmetic and copies ran while one was open for 25% of the time, Pallas kernels for 0%

commit v1 on v0

v1 whole, which is shorter than its diff:
```python
import functools

import jax
import jax.numpy as jnp
from jax import lax
from jax.experimental import pallas as pl
from jax.experimental.pallas import tpu as pltpu
from jax.sharding import PartitionSpec as P

BLK = 128
NY, NZL, NX, NZH = 8, 2, 4, 4
TOK = 128
XF = 512
CF = 256
SUB = 4
MESH = pl.DeviceIdType.MESH
F32, BF16 = jnp.float32, jnp.bfloat16


def kernel(
    cell_ref, row_ref, col_ref, count_ref, tok_ref, ct_ref, blk_ref,
    y_ref, dx_ref, bg_ref,
    xall, ctall, ctt, wd, dxb, dxl, dxz, wb, wz,
    xs, xr, cs, cr, dxs, dxr, dzs, dzr, ws, wr, wzs, wzr, gzs, gzr, gxs, gxr, gfs, gfr, gcs, gcr,
):
    d, f = lax.axis_index("dp"), lax.axis_index("fsdp")
    zh, x, c = lax.div(d, 8), lax.rem(lax.div(d, 2), 4), lax.rem(d, 2)
    y, zl = lax.div(f, 2), lax.rem(f, 2)

    def at(dzh=0, dx=0, dc=0, dy=0, dzl=0):
        nzh, nx = lax.rem(zh + dzh + NZH, NZH), lax.rem(x + dx + NX, NX)
        nc, ny, nzl = lax.rem(c + dc, 2), lax.rem(y + dy + NY, NY), lax.rem(zl + dzl, 2)
        return ((nzh * 4 + nx) * 2 + nc, ny * 2 + nzl)

    yp, ym, zp, xp, xm = at(dy=1), at(dy=-1), at(dzl=1), at(dx=1), at(dx=-1)
    core = at(dc=1)
    zhs = [None, at(dzh=1), at(dzh=2), at(dzh=3)]

    barrier = pltpu.get_barrier_semaphore()
    for peer in (yp, ym, zp, xp, xm, core, *zhs[1:]):
        pl.semaphore_signal(barrier, inc=1, device_id=peer, device_id_type=MESH)

    def remote(src, dst, ss, rs, dev):
        return pltpu.make_async_remote_copy(
            src_ref=src, dst_ref=dst, send_sem=ss, recv_sem=rs, device_id=dev, device_id_type=MESH
        )

    base = c * TOK
    for b in range(4):
        xall[4 * f + b, pl.ds(base, TOK), :] = tok_ref[:, b * BLK : (b + 1) * BLK]
    ctall[pl.ds(base, TOK), :] = ct_ref[...]
    pl.semaphore_wait(barrier, 9)

    names = {}
    sent = []

    def src_f(dy, dzl):
        return lax.rem(y + dy + NY, NY) * 2 + lax.rem(zl + dzl, 2)

    def xpart(dy, dzl, r0, n):
        return xall.at[pl.ds(4 * src_f(dy, dzl), 4), pl.ds(base + r0, n), :]

    def send(name, dy, dzl, r0, n, dev):
        k = names.setdefault(name, len(names))
        part = xpart(dy, dzl, r0, n)
        copy = remote(part, part, xs.at[k], xr.at[k], dev)
        copy.start()
        sent.append(copy)

    def recv(name, dy, dzl, r0, n):
        k = names[name]
        part = xpart(dy, dzl, r0, n)
        remote(part, part, xs.at[k], xr.at[k], core).wait_recv()

    crossed = []

    def cross(dy, dzl):
        k = len(crossed)
        part = xall.at[pl.ds(4 * src_f(dy, dzl), 4), pl.ds(base, TOK), :]
        copy = remote(part, part, cs.at[k], cr.at[k], core)
        copy.start()
        sent.append(copy)
        crossed.append((dy, dzl))

    H = TOK // 2
    send("Z0", 0, 0, H, H, zp)
    send("P0", 0, 0, 0, TOK, yp)
    send("M0", 0, 0, 0, TOK, ym)
    ctcopy = remote(ctall.at[pl.ds(base, TOK)], ctall.at[pl.ds(base, TOK)], cs.at[16], cr.at[16], core)
    ctcopy.start()
    sent.append(ctcopy)
    cross(0, 0)
    send("ZA", 0, 0, 0, H, zp)

    def build(r, carry):
        for j in range(2):
            m = cell_ref[2 * r + j]
            b = blk_ref[jnp.maximum(m, 0)]
            b = jnp.where(m >= 0, b, jnp.zeros_like(b))
            wd[pl.ds(pl.multiple_of(r * BLK, BLK), BLK), j * BLK : (j + 1) * BLK] = b
        return carry

    lax.fori_loop(0, 64, build, 0)

    recv("Z0", 0, 1, H, H)
    send("OP0", 0, 1, H, H, yp)
    send("OM0", 0, 1, H, H, ym)
    for i in (1, 2, 3):
        last = i == 3
        recv(f"P{i - 1}", -i, 0, 0, TOK)
        send(f"P{i}", -i, 0, 0, H if last else TOK, yp)
        recv(f"M{i - 1}", i, 0, 0, TOK)
        send(f"M{i}", i, 0, H if last else 0, H if last else TOK, ym)
        send(f"ZP{i}", -i, 0, 0, H, zp)
        send(f"ZM{i}", i, 0, 0, H, zp)
        cross(-i, 0)
        cross(i, 0)
        recv(f"OP{i - 1}", -i, 1, H, H)
        send(f"OP{i}", -i, 1, H, H // 2 if last else H, yp)
        recv(f"OM{i - 1}", i, 1, H, H)
        send(f"OM{i}", i, 1, H + H // 2 if last else H, H // 2 if last else H, ym)
        if i == 1:
            recv("ZA", 0, 1, 0, H)
            cross(0, 1)
        else:
            recv(f"ZP{i - 1}", -(i - 1), 1, 0, H)
            recv(f"ZM{i - 1}", i - 1, 1, 0, H)
            cross(-(i - 1), 1)
            cross(i - 1, 1)

    def dx_target(way, s):
        return lax.rem(y - 1 - s + 2 * NY, NY) if way == 0 else lax.rem(y + 1 + s, NY)

    def dx_term(way, s):
        rows = pl.multiple_of(dx_target(way, s) * (2 * XF) + way * XF, XF)
        return lax.dot_general(
            ct_ref[...], wd[pl.ds(rows, XF), :], (((1,), (1,)), ((), ())), preferred_element_type=F32
        )

    R = TOK // SUB

    def dx_copy(way, s, j):
        rows = pl.ds(pl.multiple_of(j * R, R), R)
        return remote(
            dxb.at[way, s, rows], dxb.at[way, s + 1, rows],
            dxs.at[way, s, j], dxr.at[way, s + 1, j], yp if way == 0 else ym,
        )

    def dx_wait(way, s, j):
        rows = pl.ds(pl.multiple_of(j * R, R), R)
        remote(
            dxb.at[way, s, rows], dxb.at[way, s, rows], dxs.at[way, 0, j], dxr.at[way, s, j], core
        ).wait_recv()

    def dx_part(way, s, j):
        dx_wait(way, s, j)
        rows = pl.ds(pl.multiple_of(j * R, R), R)
        dxb[way, s, rows, :] = dxb[way, s, rows, :] + dxl[way, rows, :]

    def dx_terms(s):
        for way in (0, 1):
            dxl[way] = dx_term(way, s)

    for way in (0, 1):
        dxb[way, 0] = dx_term(way, 0)

    def first(j, carry):
        for way in (0, 1):
            dx_copy(way, 0, j).start()
        return carry

    lax.fori_loop(0, SUB, first, 0)

    recv("P3", -4, 0, 0, H)
    send("ZP4", -4, 0, 0, H, zp)
    recv("M3", -4, 0, H, H)
    cross(-4, 0)
    recv("ZP3", -3, 1, 0, H)
    recv("ZM3", 3, 1, 0, H)
    cross(-3, 1)
    cross(3, 1)
    recv("OP3", -4, 1, H, H // 2)
    recv("OM3", -4, 1, H + H // 2, H // 2)
    recv("ZP4", -4, 1, 0, H)
    cross(-4, 1)

    other = lax.rem(c + 1, 2) * TOK
    part = ctall.at[pl.ds(other, TOK)]
    remote(part, part, cs.at[16], cr.at[16], core).wait_recv()
    for j in range(2):
        ctt[j] = ctall[:, j * BLK : (j + 1) * BLK].astype(F32).T.astype(BF16)
    for k, (dy, dzl) in enumerate(crossed):
        part = xall.at[pl.ds(4 * src_f(dy, dzl), 4), pl.ds(other, TOK), :]
        remote(part, part, cs.at[k], cr.at[k], core).wait_recv()

    def dw_term(tx, tzh, way):
        s = c * 32 + tx * 8 + tzh * 2 + way
        return jnp.dot(ctt[col_ref[s]], xall[row_ref[s]], preferred_element_type=F32)

    def dw_target(way, s):
        return lax.rem(x - 1 - s + 2 * NX, NX) if way == 0 else lax.rem(x + 1 + s, NX)

    def dw_copy(way, s, j):
        return remote(
            wb.at[way, s, j], wb.at[way, s + 1, j], ws.at[way, s, j], wr.at[way, s + 1, j],
            xp if way == 0 else xm,
        )

    def dw_wait(way, s, j):
        remote(wb.at[way, s, j], wb.at[way, s, j], ws.at[way, 0, j], wr.at[way, s, j], core).wait_recv()

    def part_zh(j):
        return lax.rem(zh + 1 + j, NZH)

    def dw_first(j, carry):
        for way in (0, 1):
            wb[way, 0, j] = dw_term(dw_target(way, 0), part_zh(j), way)
            dw_copy(way, 0, j).start()
        return carry

    lax.fori_loop(0, 4, dw_first, 0)

    def y_step(k, acc):
        rows = pl.ds(pl.multiple_of(k * 2 * BLK, 2 * BLK), 2 * BLK)
        xb = jnp.concatenate([xall[2 * k + b, pl.ds(base, TOK), :] for b in range(2)], axis=1)
        return acc + jnp.dot(xb, wd[rows, :], preferred_element_type=F32)

    y_ref[...] = lax.fori_loop(0, 32, y_step, jnp.zeros((TOK, CF), F32)).astype(BF16)

    for s in (1, 2):
        dx_terms(s)

        def both(j, carry, s=s):
            for way in (0, 1):
                term = dw_term(dw_target(way, s), part_zh(j), way)
                dw_wait(way, s, j)
                wb[way, s, j] = wb[way, s, j] + term
                dw_copy(way, s, j).start()
            for way in (0, 1):
                dx_part(way, s, j)
                dx_copy(way, s, j).start()
            return carry

        lax.fori_loop(0, SUB, both, 0)

    dx_terms(3)

    def wz_copy(way, j):
        return remote(wb.at[way, 3, j], wz.at[way, j], wzs.at[way, j], wzr.at[way, j], zhs[j + 1])

    for j in range(4):
        for way in (0, 1):
            term = dw_term(x, part_zh(j), way)
            dw_wait(way, 3, j)
            wb[way, 3, j] = wb[way, 3, j] + term
            if j < 3:
                wz_copy(way, j).start()
        for way in (0, 1):
            dx_part(way, 3, j)
            dx_copy(way, 3, j).start()

    def dx_round(s):
        dx_terms(s)

        def step(j, carry):
            for way in (0, 1):
                dx_part(way, s, j)
                dx_copy(way, s, j).start()
            return carry

        lax.fori_loop(0, SUB, step, 0)

    dx_round(4)

    mine = c * 32 + x * 8 + zh * 2
    for way in (0, 1):
        total = wb[way, 3, 3]
        for j in range(3):
            remote(wz.at[way, j], wz.at[way, j], wzs.at[way, j], wzr.at[way, j], core).wait_recv()
            total = total + wz[way, j]
        total = jnp.where(mine + way < count_ref[0], total.T, jnp.zeros((BLK, BLK), F32))
        bg_ref[mine + way] = total.astype(BF16)

    def slots(dx, dzh, n=2):
        return bg_ref.at[pl.ds(c * 32 + lax.rem(x + dx + NX, NX) * 8 + lax.rem(zh + dzh + NZH, NZH) * 2, n)]

    def gx_copy(way, k):
        part = slots(0, -k)
        return remote(part, part, gxs.at[way, k], gxr.at[way, k], xp if way == 0 else xm)

    for k in (1, 2, 3):
        part = slots(0, 0)
        copy = remote(part, part, gzs.at[k], gzr.at[k], zhs[k])
        copy.start()
        sent.append(copy)
    for k in range(4):
        if k:
            part = slots(0, -k)
            remote(part, part, gzs.at[k], gzr.at[k], core).wait_recv()
        for way in (0, 1):
            copy = gx_copy(way, k)
            copy.start()
            sent.append(copy)

    def whole(c_, dx):
        return bg_ref.at[pl.ds(c_ * 32 + lax.rem(x + dx + NX, NX) * 8, 8)]

    def over(k, dx):
        part = whole(c, dx)
        copy = remote(part, part, gcs.at[k], gcr.at[k], core)
        copy.start()
        sent.append(copy)

    over(0, 0)
    dx_round(5)
    for k in range(4):
        for way, dx in ((0, -1), (1, 1)):
            part = slots(dx, -k)
            remote(part, part, gxs.at[way, k], gxr.at[way, k], core).wait_recv()
            if (k < 2) == (way == 0):
                copy = remote(part, part, gfs.at[k], gfr.at[k], xp if way == 0 else xm)
                copy.start()
                sent.append(copy)
    over(1, -1)
    over(2, 1)
    dx_round(6)
    for k in range(4):
        part = slots(2, -k)
        remote(part, part, gfs.at[k], gfr.at[k], core).wait_recv()
    over(3, 2)

    dx_terms(7)

    def z_copy(j):
        rows = pl.ds(pl.multiple_of(j * R, R), R)
        return remote(dxb.at[1 - zl, 7, rows], dxz.at[rows], dzs.at[j], dzr.at[j], zp)

    for j in range(SUB):
        for way in (0, 1):
            dx_part(way, 7, j)
        z_copy(j).start()
    for j in range(SUB):
        rows = pl.ds(j * R, R)
        remote(dxz.at[rows], dxz.at[rows], dzs.at[j], dzr.at[j], core).wait_recv()
        dx_ref[rows, :] = (dxb[zl, 7, rows, :] + dxz[rows, :]).astype(BF16)

    for k, dx in enumerate((0, -1, 1, 2)):
        part = whole(1 - c, dx)
        remote(part, part, gcs.at[k], gcr.at[k], core).wait_recv()

    for copy in sent:
        copy.wait_send()
    for j in range(SUB):
        z_copy(j).wait_send()
    for way in (0, 1):
        for j in range(3):
            wz_copy(way, j).wait_send()

        def left(n, carry, way=way):
            dx_copy(way, lax.div(n, SUB), lax.rem(n, SUB)).wait_send()
            return carry

        lax.fori_loop(0, 7 * SUB, left, 0)

        def gone(n, carry, way=way):
            dw_copy(way, lax.div(n, 4), lax.rem(n, 4)).wait_send()
            return carry

        lax.fori_loop(0, 3 * 4, gone, 0)


def per_device(tokens, cotangent, blocks, slot_block, shard_count):
    row, col = slot_block // 32, slot_block % 2
    cell = row * 2 + col
    place = jnp.arange(64, dtype=jnp.int32)
    here = (cell[:, None] == jnp.arange(128, dtype=jnp.int32)[None, :]) & (place < shard_count[0])[:, None]
    cell_slot = jnp.max(jnp.where(here, place[:, None], -1), axis=0)
    smem, vmem = pl.BlockSpec(memory_space=pltpu.SMEM), pl.BlockSpec(memory_space=pltpu.VMEM)
    dma = pltpu.SemaphoreType.DMA
    return pl.pallas_call(
        kernel,
        out_shape=(
            jax.ShapeDtypeStruct((TOK, CF), BF16),
            jax.ShapeDtypeStruct((TOK, XF), BF16),
            jax.ShapeDtypeStruct((64, BLK, BLK), BF16),
        ),
        in_specs=[smem] * 4 + [vmem] * 3,
        out_specs=(vmem,) * 3,
        scratch_shapes=[
            pltpu.VMEM((64, 2 * TOK, BLK), BF16),
            pltpu.VMEM((2 * TOK, CF), BF16),
            pltpu.VMEM((2, BLK, 2 * TOK), BF16),
            pltpu.VMEM((64 * BLK, CF), BF16),
            pltpu.VMEM((2, 8, TOK, XF), F32),
            pltpu.VMEM((2, TOK, XF), F32),
            pltpu.VMEM((TOK, XF), F32),
            pltpu.VMEM((2, 4, 4, BLK, BLK), F32),
            pltpu.VMEM((2, 3, BLK, BLK), F32),
            dma((32,)), dma((32,)), dma((17,)), dma((17,)),
            dma((2, 8, SUB)), dma((2, 8, SUB)), dma((SUB,)), dma((SUB,)),
            dma((2, 4, 4)), dma((2, 4, 4)), dma((2, 3)), dma((2, 3)),
            dma((4,)), dma((4,)), dma((2, 4)), dma((2, 4)), dma((4,)), dma((4,)), dma((4,)), dma((4,)),
        ],
        compiler_params=pltpu.CompilerParams(
            collective_id=0, has_side_effects=True, vmem_limit_bytes=48 << 20
        ),
    )(cell_slot, row, col, shard_count, tokens, cotangent, blocks)


def solution(mesh):
    return jax.shard_map(
        per_device,
        mesh=mesh,
        in_specs=(P("dp", "fsdp"), P("dp", "fsdp"), P("fsdp", None, None), P("fsdp"), P("fsdp")),
        out_specs=(P("dp", "fsdp"), P("dp", "fsdp"), P("fsdp", None, None)),
        check_vma=False,
    )
```

time: 220 us -> 107 us (0.49)
  Pallas kernels: 0 us -> 98.2 us
  blocking collectives: 82.4 us -> 0 us
  waiting for transfers between devices: 47.8 us -> 0 us
  matrix products: 21.7 us -> 0 us
  local copies, waits for them, and re-layouts: 24.4 us -> 5.93 us
  starting transfers between devices: 14.7 us -> 0 us
  between operations: 14.9 us -> 1.31 us
  other arithmetic: 12.8 us -> 0.78 us
    pallas_call x0 -> x1, Pallas kernels: none -> 98.2 us  [per_device(): pl.pallas_call(kernel, out_shape=(jax.ShapeDtypeStruct((TOK, CF), BF16),...]
    all_to_all x3 -> x0, blocking collectives: 82.4 us -> none  [the longest x1 65.2 us: sum_by_axis(): return jnp.sum(lax.all_to_all(own, far, 0, 0, tiled=True), axis=0)]
    all_to_all x2 -> x0, waiting for transfers between devices: 25.5 us -> none  [copy_for_each(): return lax.all_to_all(copies, axis, split_axis=0, concat_axis=0, tiled=True)]
    dot_general x4 -> x0, matrix products: 21.7 us -> none  [the longest x1 9.14 us: apply_transposed(): lax.dot_general(g_full, band, (((1,), (1,)), ((), ())), preferred_element...]
    reduce_scatter x2 -> x0, waiting for transfers between devices: 21.6 us -> none  [sum_by_axis_2(): nearer = lax.psum_scatter(value, axes[0], scatter_dimension=dim, tiled=True)]
    all_to_all x2 -> x0, starting transfers between devices: 14.6 us -> none  [copy_for_each(): return lax.all_to_all(copies, axis, split_axis=0, concat_axis=0, tiled=True)]
    reshape x1 -> x0, local copies, waits for them, and re-layouts: 6.66 us -> none  [band_matrix(): dense = flat.astype(jnp.bfloat16).reshape(n_in, per_band, BLK, BLK)]
    gather x1 -> x0, local copies, waits for them, and re-layouts: 6.23 us -> none  [block_grads(): picked = jnp.take(tiles, cells, axis=0)]
  transfers between devices with their start and end apart: 4 -> 0, of which waited for: 2 -> 0; matrix products, arithmetic and copies ran while one was open for 25% -> 0% of each run, Pallas kernels for 0% -> 0%
where the time goes in v1:
time: 107 us; the launch traced here: 106 us
  Pallas kernels  98.2 us (92%)
  local copies, waits for them, and re-layouts  5.93 us (6%)
  between operations  1.31 us (1%)
    pallas_call x1, Pallas kernels, per_device(): pl.pallas_call(kernel, out_shape=(jax.ShapeDtypeStruct((TOK, CF), BF16),...  98.2 us
    unnamed x9, local copies, waits for them, and re-layouts  5.93 us

profile of v1, /device:TPU:1, one launch (start us, length us, event | category | flops | bytes accessed | tf_op | source)
XLA Modules:
  0.0 106.2 jit_solution(2510792838423799623)
XLA Ops:
  1.3 0.7 multiply_add_fusion
  2.0 0.1 select_reduce_fusion.cell_ref
  2.1 0.0 copy-start
  2.1 1.6 %copy-done = bf16[64,128,128]{2,1,0:T(8,128)(2,1)S(1)} copy-done((bf16[64,128,128]{2,1,0:T(8,128)(2,1)S(1)}, bf16[64,128,128]{2,1,0:T(8,128)(2,1)}, u32[]{:S(2)}) %copy-start) | copy-done | bytes 2097176
  3.7 0.0 copy-start.1
  3.7 0.9 copy-done.1
  4.6 0.0 copy-start.2
  4.6 0.8 copy-done.2
  5.4 98.2 %shard_map.76 = (bf16[128,256]{1,0:T(8,128)(2,1)S(1)}, bf16[128,512]{1,0:T(8,128)(2,1)S(1)}, bf16[64,128,128]{2,1,0:T(8,128)(2,1)S(1)}) custom-call(s32[128]{0:T(128)S(1)} %select_reduce_fusion.cell_ref, s32[64]{0:T(128)S(1)} %get-tuple-element.4.row_ref, s32[64]{0:T(128)S(1)} %get-tuple-element.5.col_ref, s32[1]{0:T(128)} %copy.11.count_ref, ...), custom_call_target="tpu_custom_call" | custom-call | tf_op jit(solution)/shard_map/pallas_call | solution.py:380
  103.6 0.6 copy.12
  104.2 0.7 copy.13
  104.9 1.3 %copy.14 = bf16[64,128,128]{2,1,0:T(8,128)(2,1)} copy(bf16[64,128,128]{2,1,0:T(8,128)(2,1)S(1)} %get-tuple-element.11) | data formatting | bytes 4194304
  (1 shorter events, 0.0 us)
Async XLA Ops:
  2.1 1.6 %copy-start = (bf16[64,128,128]{2,1,0:T(8,128)(2,1)S(1)}, bf16[64,128,128]{2,1,0:T(8,128)(2,1)}, u32[]{:S(2)}) copy-start(bf16[64,128,128]{2,1,0:T(8,128)(2,1)} %blk_ref.1) | copy-start | bytes 6291460
  3.7 0.9 copy-start.1
  4.6 0.8 copy-start.2

commit v2 on v1

v2 whole, which is shorter than its diff:
```python
import functools

import jax
import jax.numpy as jnp
from jax import lax
from jax.experimental import pallas as pl
from jax.experimental.pallas import tpu as pltpu
from jax.sharding import PartitionSpec as P

BLK = 128
NY, NZL, NX, NZH = 8, 2, 4, 4
TOK = 128
XF = 512
CF = 256
SUB = 4
MESH = pl.DeviceIdType.MESH
F32, BF16 = jnp.float32, jnp.bfloat16


CODE = 72
STEPS = 32760.0


def encode(ref, value):
    tiles = value.reshape(16, 8, BLK)
    top = jnp.max(jnp.abs(tiles), axis=0)
    power = jnp.ceil(jnp.log2(jnp.maximum(top, 1e-33)) * 8.0)
    code = jnp.round(tiles * (jnp.exp2(power * -0.125) * STEPS)[None]).astype(jnp.int32)
    pairs = lax.shift_left(code[:8], jnp.full((8, 8, BLK), 16, jnp.int32)) | (code[8:] & 0xFFFF)
    ref[0:64, :] = pairs.reshape(64, BLK)
    ref[64:CODE, :] = power.astype(jnp.int32)


def decode(ref):
    pairs = ref[0:64, :].reshape(8, 8, BLK)
    scale = jnp.exp2(ref[64:CODE, :].astype(F32) * 0.125) * (1.0 / STEPS)
    by = jnp.full((8, 8, BLK), 16, jnp.int32)
    high = lax.shift_right_arithmetic(pairs, by)
    low = lax.shift_right_arithmetic(lax.shift_left(pairs, by), by)
    tiles = jnp.concatenate([high, low], axis=0).astype(F32) * scale[None]
    return tiles.reshape(BLK, BLK)


def kernel(
    cell_ref, row_ref, col_ref, count_ref, tok_hbm, ct_hbm, blk_hbm,
    y_ref, dx_ref, bg_ref,
    xall, ctall, ctt, blk_ref, wd, yacc, dxb, dxf, dxz, wb, wf, wz,
    ls, xs, xr, cs, cr, dxs, dxr, dzs, dzr, ws, wr, wzs, wzr, gzs, gzr, gxs, gxr, gfs, gfr, gcs, gcr,
):
    d, f = lax.axis_index("dp"), lax.axis_index("fsdp")
    zh, x, c = lax.div(d, 8), lax.rem(lax.div(d, 2), 4), lax.rem(d, 2)
    y, zl = lax.div(f, 2), lax.rem(f, 2)

    def at(dzh=0, dx=0, dc=0, dy=0, dzl=0):
        nzh, nx = lax.rem(zh + dzh + NZH, NZH), lax.rem(x + dx + NX, NX)
        nc, ny, nzl = lax.rem(c + dc, 2), lax.rem(y + dy + NY, NY), lax.rem(zl + dzl, 2)
        return ((nzh * 4 + nx) * 2 + nc, ny * 2 + nzl)

    yp, ym, zp, xp, xm = at(dy=1), at(dy=-1), at(dzl=1), at(dx=1), at(dx=-1)
    core = at(dc=1)
    zhs = [None, at(dzh=1), at(dzh=2), at(dzh=3)]
    base = c * TOK

    barrier = pltpu.get_barrier_semaphore()
    for peer in (yp, ym, zp, xp, xm, core, *zhs[1:]):
        pl.semaphore_signal(barrier, inc=1, device_id=peer, device_id_type=MESH)

    loads = [
        pltpu.make_async_copy(tok_hbm.at[:, pl.ds(b * BLK, BLK)], xall.at[4 * f + b, pl.ds(base, TOK)], ls.at[b])
        for b in range(4)
    ]
    loads.append(pltpu.make_async_copy(ct_hbm, ctall.at[pl.ds(base, TOK)], ls.at[4]))
    loads.append(pltpu.make_async_copy(blk_hbm, blk_ref, ls.at[5]))
    for load in loads:
        load.start()

    def remote(src, dst, ss, rs, dev):
        return pltpu.make_async_remote_copy(
            src_ref=src, dst_ref=dst, send_sem=ss, recv_sem=rs, device_id=dev, device_id_type=MESH
        )

    names = {}
    sent = []

    def src_f(dy, dzl):
        return lax.rem(y + dy + NY, NY) * 2 + lax.rem(zl + dzl, 2)

    def xpart(dy, dzl, r0, n, start=base):
        return xall.at[pl.ds(4 * src_f(dy, dzl), 4), pl.ds(start + r0, n), :]

    def send(name, dy, dzl, r0, n, dev):
        k = names.setdefault(name, len(names))
        part = xpart(dy, dzl, r0, n)
        copy = remote(part, part, xs.at[k], xr.at[k], dev)
        copy.start()
        sent.append(copy)

    def recv(name, dy, dzl, r0, n):
        k = names[name]
        part = xpart(dy, dzl, r0, n)
        remote(part, part, xs.at[k], xr.at[k], core).wait_recv()

    crossed = []

    def cross(dy, dzl):
        k = len(crossed)
        part = xpart(dy, dzl, 0, TOK)
        copy = remote(part, part, cs.at[k], cr.at[k], core)
        copy.start()
        sent.append(copy)
        crossed.append((dy, dzl))

    H = TOK // 2
    Q = TOK // 4
    for load in loads[:5]:
        load.wait()
    pl.semaphore_wait(barrier, 9)
    send("Z0", 0, 0, H, H, zp)
    send("PA0", 0, 0, 0, H, yp)
    send("MA0", 0, 0, 0, H, ym)
    send("PB0", 0, 0, H, H, yp)
    send("MB0", 0, 0, H, H, ym)
    send("ZA", 0, 0, 0, H, zp)
    ctpart = ctall.at[pl.ds(base, TOK)]
    ctcopy = remote(ctpart, ctpart, cs.at[16], cr.at[16], core)
    ctcopy.start()
    sent.append(ctcopy)
    cross(0, 0)
    loads[5].wait()

    def build(r, carry):
        for j in range(2):
            m = cell_ref[2 * r + j]
            b = blk_ref[jnp.maximum(m, 0)]
            b = jnp.where(m >= 0, b, jnp.zeros_like(b))
            wd[pl.ds(pl.multiple_of(r * BLK, BLK), BLK), j * BLK : (j + 1) * BLK] = b
        return carry

    recv("Z0", 0, 1, H, H)
    send("OP0", 0, 1, H, H, yp)
    send("OM0", 0, 1, H, H, ym)
    for i in (1, 2, 3):
        last = i == 3
        recv(f"PA{i - 1}", -i, 0, 0, H)
        send(f"PA{i}", -i, 0, 0, H, yp)
        send(f"ZP{i}", -i, 0, 0, H, zp)
        recv(f"MA{i - 1}", i, 0, 0, H)
        if not last:
            send(f"MA{i}", i, 0, 0, H, ym)
        send(f"ZM{i}", i, 0, 0, H, zp)
        recv(f"PB{i - 1}", -i, 0, H, H)
        if not last:
            send(f"PB{i}", -i, 0, H, H, yp)
        recv(f"MB{i - 1}", i, 0, H, H)
        send(f"MB{i}", i, 0, H, H, ym)
        cross(-i, 0)
        cross(i, 0)
        recv(f"OP{i - 1}", -i, 1, H, H)
        send(f"OP{i}", -i, 1, H, Q if last else H, yp)
        recv(f"OM{i - 1}", i, 1, H, H)
        send(f"OM{i}", i, 1, H + Q if last else H, Q if last else H, ym)
        lax.fori_loop((i - 1) * 24, min(i * 24, 64), build, 0)
        if i == 1:
            recv("ZA", 0, 1, 0, H)
            cross(0, 1)
        else:
            recv(f"ZP{i - 1}", -(i - 1), 1, 0, H)
            recv(f"ZM{i - 1}", i - 1, 1, 0, H)
            cross(-(i - 1), 1)
            cross(i - 1, 1)

    def dx_target(way, s):
        return lax.rem(y - 1 - s + 2 * NY, NY) if way == 0 else lax.rem(y + 1 + s, NY)

    def dx_term(way, s, j):
        rows = pl.multiple_of(dx_target(way, s) * (2 * XF) + way * XF + j * BLK, BLK)
        return lax.dot_general(
            ctall[pl.ds(base, TOK), :], wd[pl.ds(rows, BLK), :], (((1,), (1,)), ((), ())), preferred_element_type=F32
        )

    def dx_copy(way, s, j):
        return remote(
            dxb.at[way, s, j], dxb.at[way, s + 1, j], dxs.at[way, s, j], dxr.at[way, s + 1, j],
            yp if way == 0 else ym,
        )

    def dx_part(way, s, j):
        term = dx_term(way, s, j)
        part = dxb.at[way, s, j]
        remote(part, part, dxs.at[way, 0, j], dxr.at[way, s, j], core).wait_recv()
        return term + decode(part)

    def dx_first(j, carry):
        for way in (0, 1):
            encode(dxb.at[way, 0, j], dx_term(way, 0, j))
            dx_copy(way, 0, j).start()
        return carry

    def dx_round(s):
        def step(j, carry):
            for way in (0, 1):
                encode(dxb.at[way, s, j], dx_part(way, s, j))
                dx_copy(way, s, j).start()
            return carry

        lax.fori_loop(0, SUB, step, 0)

    lax.fori_loop(0, SUB, dx_first, 0)

    recv("PA3", -4, 0, 0, H)
    send("ZP4", -4, 0, 0, H, zp)
    recv("MB3", -4, 0, H, H)
    cross(-4, 0)
    recv("ZP3", -3, 1, 0, H)
    recv("ZM3", 3, 1, 0, H)
    cross(-3, 1)
    cross(3, 1)
    recv("OP3", -4, 1, H, Q)
    recv("OM3", -4, 1, H + Q, Q)
    recv("ZP4", -4, 1, 0, H)
    cross(-4, 1)

    other = lax.rem(c + 1, 2) * TOK
    part = ctall.at[pl.ds(other, TOK)]
    remote(part, part, cs.at[16], cr.at[16], core).wait_recv()
    for j in range(2):
        ctt[j] = ctall[:, j * BLK : (j + 1) * BLK].astype(F32).T.astype(BF16)
    for k, (dy, dzl) in enumerate(crossed):
        part = xpart(dy, dzl, 0, TOK, other)
        remote(part, part, cs.at[k], cr.at[k], core).wait_recv()

    def dw_term(tx, tzh, way):
        s = c * 32 + tx * 8 + tzh * 2 + way
        return jnp.dot(ctt[col_ref[s]], xall[row_ref[s]], preferred_element_type=F32)

    def dw_target(way, s):
        return lax.rem(x - 1 - s + 2 * NX, NX) if way == 0 else lax.rem(x + 1 + s, NX)

    def dw_copy(way, s, j):
        return remote(
            wb.at[way, s, j], wb.at[way, s + 1, j], ws.at[way, s, j], wr.at[way, s + 1, j],
            xp if way == 0 else xm,
        )

    def part_zh(j):
        return lax.rem(zh + 1 + j, NZH)

    def dw_part(way, s, j):
        term = dw_term(dw_target(way, s), part_zh(j), way)
        part = wb.at[way, s, j]
        remote(part, part, ws.at[way, 0, j], wr.at[way, s, j], core).wait_recv()
        return term + decode(part)

    def dw_first(j, carry):
        for way in (0, 1):
            encode(wb.at[way, 0, j], dw_term(dw_target(way, 0), part_zh(j), way))
            dw_copy(way, 0, j).start()
        return carry

    def dw_round(s):
        def step(j, carry):
            for way in (0, 1):
                encode(wb.at[way, s, j], dw_part(way, s, j))
                dw_copy(way, s, j).start()
            return carry

        lax.fori_loop(0, 4, step, 0)

    def y_part(k):
        xb = jnp.concatenate([xall[8 * k + b, pl.ds(base, TOK), :] for b in range(8)], axis=1)
        rows = pl.ds(pl.multiple_of(k * 8 * BLK, 8 * BLK), 8 * BLK)
        term = jnp.dot(xb, wd[rows, :], preferred_element_type=F32)
        yacc[...] = term if k == 0 else yacc[...] + term

    lax.fori_loop(0, 4, dw_first, 0)
    dx_round(1)
    y_part(0)
    dw_round(1)
    y_part(1)
    dx_round(2)
    y_part(2)
    dw_round(2)
    y_part(3)
    dx_round(3)
    y_part(4)

    def wz_copy(way, j):
        return remote(wb.at[way, 0, j], wz.at[way, j], wzs.at[way, j], wzr.at[way, j], zhs[j + 1])

    for way in (0, 1):
        for j in range(3):
            dw_copy(way, 0, j).wait_send()
    for j in range(4):
        for way in (0, 1):
            total = dw_part(way, 3, j)
            if j < 3:
                encode(wb.at[way, 0, j], total)
                wz_copy(way, j).start()
            else:
                wf[way] = total
    dx_round(4)
    y_part(5)
    dx_round(5)

    mine = c * 32 + x * 8 + zh * 2
    for way in (0, 1):
        total = wf[way]
        for j in range(3):
            part = wz.at[way, j]
            remote(part, part, wzs.at[way, j], wzr.at[way, j], core).wait_recv()
            total = total + decode(part)
        total = jnp.where(mine + way < count_ref[0], total.T, jnp.zeros((BLK, BLK), F32))
        bg_ref[mine + way] = total.astype(BF16)

    def slots(dx, dzh, n=2):
        return bg_ref.at[pl.ds(c * 32 + lax.rem(x + dx + NX, NX) * 8 + lax.rem(zh + dzh + NZH, NZH) * 2, n)]

    def gx_send(k):
        part = slots(0, -k)
        for way in (0, 1):
            copy = remote(part, part, gxs.at[way, k], gxr.at[way, k], xp if way == 0 else xm)
            copy.start()
            sent.append(copy)

    def gx_pass(k):
        for way, dx in ((0, -1), (1, 1)):
            part = slots(dx, -k)
            remote(part, part, gxs.at[way, k], gxr.at[way, k], core).wait_recv()
            if (k < 2) == (way == 0):
                copy = remote(part, part, gfs.at[k], gfr.at[k], xp if way == 0 else xm)
                copy.start()
                sent.append(copy)

    def whole(c_, dx):
        return bg_ref.at[pl.ds(c_ * 32 + lax.rem(x + dx + NX, NX) * 8, 8)]

    def over(k, dx):
        part = whole(c, dx)
        copy = remote(part, part, gcs.at[k], gcr.at[k], core)
        copy.start()
        sent.append(copy)

    gx_send(0)
    for k in (1, 2, 3):
        part = slots(0, 0)
        copy = remote(part, part, gzs.at[k], gzr.at[k], zhs[k])
        copy.start()
        sent.append(copy)
    dx_round(6)
    for k in (1, 3, 2):
        part = slots(0, -k)
        remote(part, part, gzs.at[k], gzr.at[k], core).wait_recv()
        gx_send(k)
    over(0, 0)
    gx_pass(0)

    def z_copy(j):
        return remote(dxb.at[1 - zl, 0, j], dxz.at[j], dzs.at[j], dzr.at[j], zp)

    for way in (0, 1):
        for j in range(SUB):
            dx_copy(way, 0, j).wait_send()
    for j in range(SUB):
        for way in (0, 1):
            dxf[way, j] = dx_part(way, 7, j)
        encode(dxb.at[1 - zl, 0, j], dxf[1 - zl, j])
        z_copy(j).start()
    y_part(6)
    gx_pass(1)
    y_part(7)
    y_ref[...] = yacc[...].astype(BF16)
    gx_pass(3)
    gx_pass(2)
    over(1, -1)
    over(2, 1)
    for j in range(SUB):
        part = dxz.at[j]
        remote(part, part, dzs.at[j], dzr.at[j], core).wait_recv()
        dx_ref[:, j * BLK : (j + 1) * BLK] = (dxf[zl, j] + decode(part)).astype(BF16)
    for k in range(4):
        part = slots(2, -k)
        remote(part, part, gfs.at[k], gfr.at[k], core).wait_recv()
    over(3, 2)
    for k, dx in enumerate((0, -1, 1, 2)):
        part = whole(1 - c, dx)
        remote(part, part, gcs.at[k], gcr.at[k], core).wait_recv()

    for copy in sent:
        copy.wait_send()
    for j in range(SUB):
        z_copy(j).wait_send()
    for way in (0, 1):
        for j in range(3):
            wz_copy(way, j).wait_send()
        dw_copy(way, 0, 3).wait_send()

        def left(n, carry, way=way):
            dx_copy(way, lax.div(n, SUB), lax.rem(n, SUB)).wait_send()
            return carry

        lax.fori_loop(SUB, 7 * SUB, left, 0)

        def gone(n, carry, way=way):
            dw_copy(way, lax.div(n, 4), lax.rem(n, 4)).wait_send()
            return carry

        lax.fori_loop(4, 3 * 4, gone, 0)


def per_device(tokens, cotangent, blocks, slot_block, shard_count):
    row, col = slot_block // 32, slot_block % 2
    cell = row * 2 + col
    place = jnp.arange(64, dtype=jnp.int32)
    here = (cell[:, None] == jnp.arange(128, dtype=jnp.int32)[None, :]) & (place < shard_count[0])[:, None]
    cell_slot = jnp.max(jnp.where(here, place[:, None], -1), axis=0)
    smem, vmem, hbm = (pl.BlockSpec(memory_space=m) for m in (pltpu.SMEM, pltpu.VMEM, pltpu.HBM))
    dma = pltpu.SemaphoreType.DMA
    return pl.pallas_call(
        kernel,
        out_shape=(
            jax.ShapeDtypeStruct((TOK, CF), BF16),
            jax.ShapeDtypeStruct((TOK, XF), BF16),
            jax.ShapeDtypeStruct((64, BLK, BLK), BF16),
        ),
        in_specs=[smem] * 4 + [hbm] * 3,
        out_specs=(vmem,) * 3,
        scratch_shapes=[
            pltpu.VMEM((64, 2 * TOK, BLK), BF16),
            pltpu.VMEM((2 * TOK, CF), BF16),
            pltpu.VMEM((2, BLK, 2 * TOK), BF16),
            pltpu.VMEM((64, BLK, BLK), BF16),
            pltpu.VMEM((64 * BLK, CF), BF16),
            pltpu.VMEM((TOK, CF), F32),
            pltpu.VMEM((2, 8, SUB, CODE, BLK), jnp.int32),
            pltpu.VMEM((2, SUB, BLK, BLK), F32),
            pltpu.VMEM((SUB, CODE, BLK), jnp.int32),
            pltpu.VMEM((2, 4, 4, CODE, BLK), jnp.int32),
            pltpu.VMEM((2, BLK, BLK), F32),
            pltpu.VMEM((2, 3, CODE, BLK), jnp.int32),
            dma((6,)), dma((40,)), dma((40,)), dma((17,)), dma((17,)),
            dma((2, 8, SUB)), dma((2, 8, SUB)), dma((SUB,)), dma((SUB,)),
            dma((2, 4, 4)), dma((2, 4, 4)), dma((2, 3)), dma((2, 3)),
            dma((4,)), dma((4,)), dma((2, 4)), dma((2, 4)), dma((4,)), dma((4,)), dma((4,)), dma((4,)),
        ],
        compiler_params=pltpu.CompilerParams(
            collective_id=0, has_side_effects=True, vmem_limit_bytes=48 << 20
        ),
    )(cell_slot, row, col, shard_count, tokens, cotangent, blocks)


def solution(mesh):
    return jax.shard_map(
        per_device,
        mesh=mesh,
        in_specs=(P("dp", "fsdp"), P("dp", "fsdp"), P("fsdp", None, None), P("fsdp"), P("fsdp")),
        out_specs=(P("dp", "fsdp"), P("dp", "fsdp"), P("fsdp", None, None)),
        check_vma=False,
    )
```

time: 107 us -> 90.5 us (0.85)
  Pallas kernels: 98.2 us -> 81.8 us
    pallas_call x1, Pallas kernels: 98.2 us -> 81.8 us  [per_device(): pl.pallas_call(kernel, out_shape=(jax.ShapeDtypeStruct((TOK, CF), BF16),...]
where the time goes in v2:
time: 90.5 us; the launch traced here: 89.8 us
  Pallas kernels  81.8 us (90%)
  local copies, waits for them, and re-layouts  5.93 us (7%)
  between operations  1.31 us (1%)
    pallas_call x1, Pallas kernels, per_device(): pl.pallas_call(kernel, out_shape=(jax.ShapeDtypeStruct((TOK, CF), BF16),...  81.8 us
    unnamed x9, local copies, waits for them, and re-layouts  5.93 us

profile of v2, /device:TPU:1, one launch (start us, length us, event | category | flops | bytes accessed | tf_op | source)
XLA Modules:
  0.0 89.8 jit_solution(7445129400745726485)
XLA Ops:
  1.3 0.7 multiply_add_fusion
  2.0 0.1 select_reduce_fusion.cell_ref
  2.1 0.0 copy-start
  2.1 1.6 %copy-done = bf16[64,128,128]{2,1,0:T(8,128)(2,1)S(1)} copy-done((bf16[64,128,128]{2,1,0:T(8,128)(2,1)S(1)}, bf16[64,128,128]{2,1,0:T(8,128)(2,1)}, u32[]{:S(2)}) %copy-start) | copy-done | bytes 2097176
  3.7 0.0 copy-start.1
  3.7 0.9 %copy-done.1 = bf16[128,512]{1,0:T(8,128)(2,1)S(1)} copy-done((bf16[128,512]{1,0:T(8,128)(2,1)S(1)}, bf16[128,512]{1,0:T(8,128)(2,1)}, u32[]{:S(2)}) %copy-start.1) | copy-done | bytes 131096
  4.6 0.0 copy-start.2
  4.6 0.8 copy-done.2
  5.4 81.8 %shard_map.76 = (bf16[128,256]{1,0:T(8,128)(2,1)S(1)}, bf16[128,512]{1,0:T(8,128)(2,1)S(1)}, bf16[64,128,128]{2,1,0:T(8,128)(2,1)S(1)}) custom-call(s32[128]{0:T(128)S(1)} %select_reduce_fusion.cell_ref, s32[64]{0:T(128)S(1)} %get-tuple-element.4.row_ref, s32[64]{0:T(128)S(1)} %get-tuple-element.5.col_ref, s32[1]{0:T(128)} %copy.11.count_ref, ...), custom_call_target="tpu_custom_call" | custom-call | tf_op jit(solution)/shard_map/pallas_call | solution.py:418
  87.2 0.6 copy.12
  87.8 0.7 copy.13
  88.5 1.3 %copy.14 = bf16[64,128,128]{2,1,0:T(8,128)(2,1)} copy(bf16[64,128,128]{2,1,0:T(8,128)(2,1)S(1)} %get-tuple-element.11) | data formatting | bytes 4194304
  (1 shorter events, 0.0 us)
Async XLA Ops:
  2.1 1.6 %copy-start = (bf16[64,128,128]{2,1,0:T(8,128)(2,1)S(1)}, bf16[64,128,128]{2,1,0:T(8,128)(2,1)}, u32[]{:S(2)}) copy-start(bf16[64,128,128]{2,1,0:T(8,128)(2,1)} %blk_hbm.1) | copy-start | bytes 6291460
  3.7 0.9 %copy-start.1 = (bf16[128,512]{1,0:T(8,128)(2,1)S(1)}, bf16[128,512]{1,0:T(8,128)(2,1)}, u32[]{:S(2)}) copy-start(bf16[128,512]{1,0:T(8,128)(2,1)} %tok_hbm.1) | copy-start | bytes 393220
  4.6 0.8 copy-start.2

commit v3 on v2

v3 whole, which is shorter than its diff:
```python
import functools

import jax
import jax.numpy as jnp
from jax import lax
from jax.experimental import pallas as pl
from jax.experimental.pallas import tpu as pltpu
from jax.sharding import PartitionSpec as P

BLK = 128
NY, NZL, NX, NZH = 8, 2, 4, 4
TOK = 128
XF = 512
CF = 256
SUB = 4
MESH = pl.DeviceIdType.MESH
F32, BF16 = jnp.float32, jnp.bfloat16


CODE = 72
STEPS = 32760.0


def encode(ref, value):
    tiles = value.reshape(16, 8, BLK)
    top = jnp.max(jnp.abs(tiles), axis=0)
    power = jnp.ceil(jnp.log2(jnp.maximum(top, 1e-33)) * 8.0)
    code = jnp.round(tiles * (jnp.exp2(power * -0.125) * STEPS)[None]).astype(jnp.int32)
    pairs = lax.shift_left(code[:8], jnp.full((8, 8, BLK), 16, jnp.int32)) | (code[8:] & 0xFFFF)
    ref[0:64, :] = pairs.reshape(64, BLK)
    ref[64:CODE, :] = power.astype(jnp.int32)


def decode(ref):
    pairs = ref[0:64, :].reshape(8, 8, BLK)
    scale = jnp.exp2(ref[64:CODE, :].astype(F32) * 0.125) * (1.0 / STEPS)
    by = jnp.full((8, 8, BLK), 16, jnp.int32)
    high = lax.shift_right_arithmetic(pairs, by)
    low = lax.shift_right_arithmetic(lax.shift_left(pairs, by), by)
    tiles = jnp.concatenate([high, low], axis=0).astype(F32) * scale[None]
    return tiles.reshape(BLK, BLK)


def kernel(
    table_ref, tok_hbm, ct_hbm, blk_hbm,
    y_ref, dx_ref, bg_ref,
    xall, ctall, ctt, blk_ref, wd, yacc, dxt, dxb, dxf, dxz, wsb, wrb, wf, zsb, zrb, bgv, youtv, dxv,
    ls, xs, xr, cs, cr, dxs, dxr, dzs, dzr, ws, wr, wzs, wzr, gzs, gzr, gxs, gxr, gfs, gfr, gcs, gcr, os,
):
    d, f = lax.axis_index("dp"), lax.axis_index("fsdp")
    zh, x, c = lax.div(d, 8), lax.rem(lax.div(d, 2), 4), lax.rem(d, 2)
    y, zl = lax.div(f, 2), lax.rem(f, 2)

    def at(dzh=0, dx=0, dc=0, dy=0, dzl=0):
        nzh, nx = lax.rem(zh + dzh + NZH, NZH), lax.rem(x + dx + NX, NX)
        nc, ny, nzl = lax.rem(c + dc, 2), lax.rem(y + dy + NY, NY), lax.rem(zl + dzl, 2)
        return ((nzh * 4 + nx) * 2 + nc, ny * 2 + nzl)

    yp, ym, zp, xp, xm = at(dy=1), at(dy=-1), at(dzl=1), at(dx=1), at(dx=-1)
    core = at(dc=1)
    zhs = [None, at(dzh=1), at(dzh=2), at(dzh=3)]
    xs_to = [xp, at(dx=2), xm]
    base = c * TOK

    barrier = pltpu.get_barrier_semaphore()
    for peer in (yp, ym, zp, *xs_to, core, *zhs[1:]):
        pl.semaphore_signal(barrier, inc=1, device_id=peer, device_id_type=MESH)

    loads = [
        pltpu.make_async_copy(tok_hbm.at[:, pl.ds(b * BLK, BLK)], xall.at[4 * f + b, pl.ds(base, TOK)], ls.at[b])
        for b in range(4)
    ]
    loads.append(pltpu.make_async_copy(ct_hbm, ctall.at[pl.ds(base, TOK)], ls.at[4]))
    loads.append(pltpu.make_async_copy(blk_hbm, blk_ref, ls.at[5]))
    for load in loads:
        load.start()

    def remote(src, dst, ss, rs, dev):
        return pltpu.make_async_remote_copy(
            src_ref=src, dst_ref=dst, send_sem=ss, recv_sem=rs, device_id=dev, device_id_type=MESH
        )

    names = {}
    sent = []

    def src_f(dy, dzl):
        return lax.rem(y + dy + NY, NY) * 2 + lax.rem(zl + dzl, 2)

    def xpart(dy, dzl, r0, n, start=base):
        return xall.at[pl.ds(4 * src_f(dy, dzl), 4), pl.ds(start + r0, n), :]

    def send(name, dy, dzl, r0, n, dev):
        k = names.setdefault(name, len(names))
        part = xpart(dy, dzl, r0, n)
        copy = remote(part, part, xs.at[k], xr.at[k], dev)
        copy.start()
        sent.append(copy)

    def recv(name, dy, dzl, r0, n):
        k = names[name]
        part = xpart(dy, dzl, r0, n)
        remote(part, part, xs.at[k], xr.at[k], core).wait_recv()

    crossed = []

    def cross(dy, dzl):
        k = len(crossed)
        part = xpart(dy, dzl, 0, TOK)
        copy = remote(part, part, cs.at[k], cr.at[k], core)
        copy.start()
        sent.append(copy)
        crossed.append((dy, dzl))

    H = TOK // 2
    Q = TOK // 4
    for load in loads[:5]:
        load.wait()
    pl.semaphore_wait(barrier, 10)
    send("Z0", 0, 0, H, H, zp)
    send("PA0", 0, 0, 0, H, yp)
    send("MA0", 0, 0, 0, H, ym)
    send("PB0", 0, 0, H, H, yp)
    send("MB0", 0, 0, H, H, ym)
    send("ZA", 0, 0, 0, H, zp)
    ctpart = ctall.at[pl.ds(base, TOK)]
    ctcopy = remote(ctpart, ctpart, cs.at[16], cr.at[16], core)
    ctcopy.start()
    sent.append(ctcopy)
    cross(0, 0)
    loads[5].wait()

    def build(r, carry):
        for j in range(2):
            m = table_ref[2 * r + j]
            b = blk_ref[jnp.maximum(m, 0)]
            b = jnp.where(m >= 0, b, jnp.zeros_like(b))
            wd[pl.ds(pl.multiple_of(r * BLK, BLK), BLK), j * BLK : (j + 1) * BLK] = b
        return carry

    def dx_target(way, s):
        return lax.rem(y - 1 - s + 2 * NY, NY) if way == 0 else lax.rem(y + 1 + s, NY)

    def dx_terms(s):
        for way in (0, 1):
            rows = pl.multiple_of(dx_target(way, s) * (2 * XF) + way * XF, XF)
            terms = lax.dot_general(
                ctall[pl.ds(base, TOK), :], wd[pl.ds(rows, XF), :], (((1,), (1,)), ((), ())), preferred_element_type=F32
            )
            for j in range(SUB):
                dxt[way, s, j] = terms[:, j * BLK : (j + 1) * BLK]

    def dx_copy(way, s, j):
        return remote(
            dxb.at[way, s, j], dxb.at[way, s + 1, j], dxs.at[way, s, j], dxr.at[way, s + 1, j],
            yp if way == 0 else ym,
        )

    def dx_part(way, s, j):
        part = dxb.at[way, s, j]
        remote(part, part, dxs.at[way, 0, j], dxr.at[way, s, j], core).wait_recv()
        return dxt[way, s, j] + decode(part)

    def dx_first(j, carry):
        for way in (0, 1):
            encode(dxb.at[way, 0, j], dxt[way, 0, j])
            dx_copy(way, 0, j).start()
        return carry

    def dx_round(s):
        def step(j, carry):
            for way in (0, 1):
                encode(dxb.at[way, s, j], dx_part(way, s, j))
                dx_copy(way, s, j).start()
            return carry

        lax.fori_loop(0, SUB, step, 0)

    def y_part(dy, dzl, first=False):
        k = src_f(dy, dzl)
        xb = jnp.concatenate([xall[4 * k + b, pl.ds(base, TOK), :] for b in range(4)], axis=1)
        rows = pl.ds(pl.multiple_of(k * XF, XF), XF)
        term = jnp.dot(xb, wd[rows, :], preferred_element_type=F32)
        yacc[...] = term if first else yacc[...] + term

    lax.fori_loop(0, 64, build, 0)
    y_part(0, 0, True)
    recv("Z0", 0, 1, H, H)
    send("OP0", 0, 1, H, H, yp)
    send("OM0", 0, 1, H, H, ym)
    dx_terms(0)
    for i in (1, 2, 3):
        last = i == 3
        recv(f"PA{i - 1}", -i, 0, 0, H)
        send(f"PA{i}", -i, 0, 0, H, yp)
        send(f"ZP{i}", -i, 0, 0, H, zp)
        recv(f"MA{i - 1}", i, 0, 0, H)
        if not last:
            send(f"MA{i}", i, 0, 0, H, ym)
        send(f"ZM{i}", i, 0, 0, H, zp)
        recv(f"PB{i - 1}", -i, 0, H, H)
        if not last:
            send(f"PB{i}", -i, 0, H, H, yp)
        recv(f"MB{i - 1}", i, 0, H, H)
        send(f"MB{i}", i, 0, H, H, ym)
        cross(-i, 0)
        cross(i, 0)
        recv(f"OP{i - 1}", -i, 1, H, H)
        send(f"OP{i}", -i, 1, H, Q if last else H, yp)
        recv(f"OM{i - 1}", i, 1, H, H)
        send(f"OM{i}", i, 1, H + Q if last else H, Q if last else H, ym)
        if i == 1:
            dx_terms(1)
            recv("ZA", 0, 1, 0, H)
            cross(0, 1)
            y_part(0, 1)
            y_part(-1, 0)
        elif i == 2:
            recv("ZP1", -1, 1, 0, H)
            recv("ZM1", 1, 1, 0, H)
            cross(-1, 1)
            cross(1, 1)
            y_part(1, 0)
            dx_terms(2)
            dx_terms(3)
        else:
            lax.fori_loop(0, SUB, dx_first, 0)
            recv("ZP2", -2, 1, 0, H)
            recv("ZM2", 2, 1, 0, H)
            cross(-2, 1)
            cross(2, 1)
            y_part(-1, 1)
            y_part(1, 1)

    recv("PA3", -4, 0, 0, H)
    send("ZP4", -4, 0, 0, H, zp)
    recv("MB3", -4, 0, H, H)
    cross(-4, 0)
    dx_terms(4)
    recv("ZP3", -3, 1, 0, H)
    recv("ZM3", 3, 1, 0, H)
    cross(-3, 1)
    cross(3, 1)
    recv("OP3", -4, 1, H, Q)
    recv("OM3", -4, 1, H + Q, Q)
    dx_terms(5)
    other = lax.rem(c + 1, 2) * TOK
    part = ctall.at[pl.ds(other, TOK)]
    remote(part, part, cs.at[16], cr.at[16], core).wait_recv()
    for j in range(2):
        ctt[j] = ctall[:, j * BLK : (j + 1) * BLK].astype(F32).T.astype(BF16)
    y_part(-2, 0)
    recv("ZP4", -4, 1, 0, H)
    cross(-4, 1)
    dx_round(1)
    y_part(2, 0)

    for k, (dy, dzl) in enumerate(crossed):
        part = xpart(dy, dzl, 0, TOK, other)
        remote(part, part, cs.at[k], cr.at[k], core).wait_recv()
    from_gather = len(sent)

    def dw_term(tx, tzh, way):
        s = c * 32 + tx * 8 + tzh * 2 + way
        slot = table_ref[128 + s]
        return jnp.dot(ctt[slot & 1], xall[lax.shift_right_logical(slot, 5)], preferred_element_type=F32)

    def part_off(j):
        return lax.rem(2 + 3 * j - lax.div(j * (j - 1), 2), NZH)

    def dw_copy(o, j):
        return remote(wsb.at[o, j], wrb.at[o, j], ws.at[o, j], wr.at[o, j], xs_to[o])

    def dw_send(j, carry):
        tzh = lax.rem(zh + part_off(j), NZH)
        for o in (1, 0, 2):
            for i in range(2):
                encode(wsb.at[o, j, i], dw_term(lax.rem(x + o + 1, NX), tzh, i))
            dw_copy(o, j).start()
        return carry

    def wz_copy(j):
        return remote(zsb.at[j], zrb.at[j], wzs.at[j], wzr.at[j], zhs[(2, 1, 3)[j]])

    def dw_sum(j):
        tzh = lax.rem(zh + (2, 1, 3, 0)[j], NZH)
        for o in range(3):
            part = wrb.at[o, j]
            remote(part, part, ws.at[o, j], wr.at[o, j], core).wait_recv()
        for i in range(2):
            total = dw_term(x, tzh, i)
            for o in range(3):
                total = total + decode(wrb.at[o, j, i])
            if j < 3:
                encode(zsb.at[j, i], total)
            else:
                wf[i] = total
        if j < 3:
            wz_copy(j).start()

    lax.fori_loop(0, 4, dw_send, 0)
    dx_round(2)
    y_part(-3, 0)
    dw_sum(0)
    dx_round(3)
    dw_sum(1)
    dx_terms(6)
    dw_sum(2)
    dx_round(4)
    dw_sum(3)
    dx_terms(7)
    y_part(-4, 0)
    y_part(3, 0)
    dx_round(5)

    mine = c * 32 + x * 8 + zh * 2
    for j in (1, 2, 0):
        part = zrb.at[j]
        remote(part, part, wzs.at[j], wzr.at[j], core).wait_recv()
    for i in range(2):
        total = wf[i]
        for j in range(3):
            total = total + decode(zrb.at[j, i])
        total = jnp.where(mine + i < table_ref[192], total.T, jnp.zeros((BLK, BLK), F32))
        bgv[mine + i] = total.astype(BF16)

    def slots(dx, dzh, n=2, half=c):
        return bgv.at[pl.ds(half * 32 + lax.rem(x + dx + NX, NX) * 8 + lax.rem(zh + dzh + NZH, NZH) * 2, n)]

    def put(part, ss, rs, dev):
        copy = remote(part, part, ss, rs, dev)
        copy.start()
        sent.append(copy)

    def over(m, k):
        put(slots((0, -1, 1, 2)[m], -k), gcs.at[m, k], gcr.at[m, k], core)

    def gx_send(k):
        for way in (0, 1):
            put(slots(0, -k), gxs.at[way, k], gxr.at[way, k], xp if way == 0 else xm)

    def gx_pass(k):
        for way, dx in ((0, -1), (1, 1)):
            part = slots(dx, -k)
            remote(part, part, gxs.at[way, k], gxr.at[way, k], core).wait_recv()
            if (k in (0, 1)) == (way == 0):
                put(part, gfs.at[k], gfr.at[k], xp if way == 0 else xm)
            over(1 + way, k)

    def gf_take(k):
        part = slots(2, -k)
        remote(part, part, gfs.at[k], gfr.at[k], core).wait_recv()
        over(3, k)

    def write(half, m):
        part = pl.ds(half * 32 + lax.rem(x + (0, -1, 1, 2)[m] + NX, NX) * 8, 8)
        return pltpu.make_async_copy(bgv.at[part], bg_ref.at[part], os.at[(0 if half is c else 4) + m])

    for k in (2, 1, 3):
        put(slots(0, 0), gzs.at[k], gzr.at[k], zhs[k])
    gx_send(0)
    over(0, 0)
    for copy in sent[:from_gather]:
        copy.wait_send()
    dx_round(6)
    for k in (1, 3, 2):
        part = slots(0, -k)
        remote(part, part, gzs.at[k], gzr.at[k], core).wait_recv()
        gx_send(k)
        over(0, k)
        if k == 1:
            gx_pass(0)
    write(c, 0).start()

    def z_copy(j):
        return remote(dxb.at[1 - zl, 0, j], dxz.at[j], dzs.at[j], dzr.at[j], zp)

    for way in (0, 1):
        for j in range(SUB):
            dx_copy(way, 0, j).wait_send()
    for j in range(SUB):
        for way in (0, 1):
            dxf[way, j] = dx_part(way, 7, j)
        encode(dxb.at[1 - zl, 0, j], dxf[1 - zl, j])
        z_copy(j).start()
    gx_pass(1)
    gx_pass(3)
    y_part(-2, 1)
    y_part(2, 1)
    gx_pass(2)
    write(c, 1).start()
    write(c, 2).start()
    y_part(-3, 1)
    y_part(3, 1)
    y_part(-4, 1)
    youtv[...] = yacc[...].astype(BF16)
    ywrite = pltpu.make_async_copy(youtv, y_ref, os.at[8])
    ywrite.start()
    for j in range(SUB):
        part = dxz.at[j]
        remote(part, part, dzs.at[j], dzr.at[j], core).wait_recv()
        dxv[:, j * BLK : (j + 1) * BLK] = (dxf[zl, j] + decode(part)).astype(BF16)
    dxwrite = pltpu.make_async_copy(dxv, dx_ref, os.at[9])
    dxwrite.start()
    for k in (0, 1, 3, 2):
        gf_take(k)
    write(c, 3).start()
    for m in range(4):
        for k in range(4):
            part = slots((0, -1, 1, 2)[m], -k, 2, 1 - c)
            remote(part, part, gcs.at[m, k], gcr.at[m, k], core).wait_recv()
        write(1 - c, m).start()

    for copy in sent[from_gather:]:
        copy.wait_send()
    for j in range(SUB):
        z_copy(j).wait_send()
    for j in range(3):
        wz_copy(j).wait_send()

    for way in (0, 1):

        def left(n, carry, way=way):
            dx_copy(way, lax.div(n, SUB), lax.rem(n, SUB)).wait_send()
            return carry

        lax.fori_loop(SUB, 7 * SUB, left, 0)
    for o in range(3):

        def gone(j, carry, o=o):
            dw_copy(o, j).wait_send()
            return carry

        lax.fori_loop(0, 4, gone, 0)
    for m in range(4):
        write(c, m).wait()
        write(1 - c, m).wait()
    ywrite.wait()
    dxwrite.wait()


def per_device(tokens, cotangent, blocks, slot_block, shard_count):
    cell = slot_block // 32 * 2 + slot_block % 2
    place = jnp.arange(64, dtype=jnp.int32)
    here = (cell[:, None] == jnp.arange(128, dtype=jnp.int32)[None, :]) & (place < shard_count[0])[:, None]
    cell_slot = jnp.max(jnp.where(here, place[:, None], -1), axis=0)
    table = jnp.concatenate([cell_slot, slot_block, shard_count])
    smem, hbm = pl.BlockSpec(memory_space=pltpu.SMEM), pl.BlockSpec(memory_space=pltpu.HBM)
    dma = pltpu.SemaphoreType.DMA
    return pl.pallas_call(
        kernel,
        out_shape=(
            jax.ShapeDtypeStruct((TOK, CF), BF16),
            jax.ShapeDtypeStruct((TOK, XF), BF16),
            jax.ShapeDtypeStruct((64, BLK, BLK), BF16),
        ),
        in_specs=[smem] + [hbm] * 3,
        out_specs=(hbm,) * 3,
        scratch_shapes=[
            pltpu.VMEM((64, 2 * TOK, BLK), BF16),
            pltpu.VMEM((2 * TOK, CF), BF16),
            pltpu.VMEM((2, BLK, 2 * TOK), BF16),
            pltpu.VMEM((64, BLK, BLK), BF16),
            pltpu.VMEM((64 * BLK, CF), BF16),
            pltpu.VMEM((TOK, CF), F32),
            pltpu.VMEM((2, 8, SUB, BLK, BLK), F32),
            pltpu.VMEM((2, 8, SUB, CODE, BLK), jnp.int32),
            pltpu.VMEM((2, SUB, BLK, BLK), F32),
            pltpu.VMEM((SUB, CODE, BLK), jnp.int32),
            pltpu.VMEM((3, 4, 2, CODE, BLK), jnp.int32),
            pltpu.VMEM((3, 4, 2, CODE, BLK), jnp.int32),
            pltpu.VMEM((2, BLK, BLK), F32),
            pltpu.VMEM((3, 2, CODE, BLK), jnp.int32),
            pltpu.VMEM((3, 2, CODE, BLK), jnp.int32),
            pltpu.VMEM((64, BLK, BLK), BF16),
            pltpu.VMEM((TOK, CF), BF16),
            pltpu.VMEM((TOK, XF), BF16),
            dma((6,)), dma((40,)), dma((40,)), dma((17,)), dma((17,)),
            dma((2, 8, SUB)), dma((2, 8, SUB)), dma((SUB,)), dma((SUB,)),
            dma((3, 4)), dma((3, 4)), dma((3,)), dma((3,)),
            dma((4,)), dma((4,)), dma((2, 4)), dma((2, 4)), dma((4,)), dma((4,)), dma((4, 4)), dma((4, 4)), dma((10,)),
        ],
        compiler_params=pltpu.CompilerParams(
            collective_id=0, has_side_effects=True, vmem_limit_bytes=50 << 20
        ),
    )(table, tokens, cotangent, blocks)


def solution(mesh):
    return jax.shard_map(
        per_device,
        mesh=mesh,
        in_specs=(P("dp", "fsdp"), P("dp", "fsdp"), P("fsdp", None, None), P("fsdp"), P("fsdp")),
        out_specs=(P("dp", "fsdp"), P("dp", "fsdp"), P("fsdp", None, None)),
        check_vma=False,
    )
```

time: 90.5 us -> 84.7 us (0.936)
  Pallas kernels: 81.8 us -> 77.3 us
  local copies, waits for them, and re-layouts: 5.93 us -> 4.35 us
    pallas_call x1, Pallas kernels: 81.8 us -> 77.3 us  [per_device(): pl.pallas_call(kernel, out_shape=(jax.ShapeDtypeStruct((TOK, CF), BF16),...]
    unnamed x9 -> x7, local copies, waits for them, and re-layouts: 5.93 us -> 4.35 us
where the time goes in v3:
time: 84.7 us; the launch traced here: 84.5 us
  Pallas kernels  77.3 us (91%)
  local copies, waits for them, and re-layouts  4.35 us (5%)
  other arithmetic  1.51 us (2%)
  between operations  1.29 us (2%)
    pallas_call x1, Pallas kernels, per_device(): pl.pallas_call(kernel, out_shape=(jax.ShapeDtypeStruct((TOK, CF), BF16),...  77.3 us
    unnamed x7, local copies, waits for them, and re-layouts  4.35 us

profile of v3, /device:TPU:1, one launch (start us, length us, event | category | flops | bytes accessed | tf_op | source)
XLA Modules:
  0.0 84.5 jit_solution(16279559978941304304)
XLA Ops:
  1.3 0.7 fusion.1
  2.0 0.1 select_reduce_fusion
  2.1 0.7 pad_add_fusion.table_ref
  2.8 0.0 copy-start
  2.8 0.9 %copy-done = bf16[128,512]{1,0:T(8,128)(2,1)S(1)} copy-done((bf16[128,512]{1,0:T(8,128)(2,1)S(1)}, bf16[128,512]{1,0:T(8,128)(2,1)}, u32[]{:S(2)}) %copy-start) | copy-done | bytes 131096
  3.7 0.0 copy-start.1
  3.7 0.8 copy-done.1
  4.5 77.3 %shard_map.76 = (bf16[128,256]{1,0:T(8,128)(2,1)S(1)}, bf16[128,512]{1,0:T(8,128)(2,1)S(1)}, bf16[64,128,128]{2,1,0:T(8,128)(2,1)S(1)}) custom-call(s32[193]{0:T(256)S(1)} %pad_add_fusion.table_ref, bf16[128,512]{1,0:T(8,128)(2,1)S(1)} %copy-done, bf16[128,256]{1,0:T(8,128)(2,1)S(1)} %copy-done.1, bf16[64,128,128]{2,1,0:T(8,128)(2,1)} %blk_hbm.1), custom_call_target="tpu_custom_call" | custom-call | tf_op jit(solution)/shard_map/pallas_call | solution.py:449
  81.8 0.6 copy.12
  82.5 0.7 copy.13
  83.1 1.3 %copy.14 = bf16[64,128,128]{2,1,0:T(8,128)(2,1)} copy(bf16[64,128,128]{2,1,0:T(8,128)(2,1)S(1)} %get-tuple-element.8) | data formatting | bytes 4194304
  (1 shorter events, 0.0 us)
Async XLA Ops:
  2.8 0.9 %copy-start = (bf16[128,512]{1,0:T(8,128)(2,1)S(1)}, bf16[128,512]{1,0:T(8,128)(2,1)}, u32[]{:S(2)}) copy-start(bf16[128,512]{1,0:T(8,128)(2,1)} %tok_hbm.1) | copy-start | bytes 393220
  3.7 0.8 copy-start.1

commit v4 on v3

--- a/solution.py
+++ b/solution.py
@@ -44,8 +44,8 @@
 def kernel(
     table_ref, tok_hbm, ct_hbm, blk_hbm,
     y_ref, dx_ref, bg_ref,
-    xall, ctall, ctt, blk_ref, wd, yacc, dxt, dxb, dxf, dxz, wsb, wrb, wf, zsb, zrb, bgv, youtv, dxv,
-    ls, xs, xr, cs, cr, dxs, dxr, dzs, dzr, ws, wr, wzs, wzr, gzs, gzr, gxs, gxr, gfs, gfr, gcs, gcr, os,
+    xall, ctall, ctt, blk_ref, wd, yacc, dxt, dxb, dxf, dxz, wsb, wrb, wf, zsb, zrb,
+    ls, xs, xr, cs, cr, dxs, dxr, dzs, dzr, ws, wr, wzs, wzr, gzs, gzr, gxs, gxr, gfs, gfr, gcs, gcr,
 ):
     d, f = lax.axis_index("dp"), lax.axis_index("fsdp")
     zh, x, c = lax.div(d, 8), lax.rem(lax.div(d, 2), 4), lax.rem(d, 2)
@@ -321,10 +321,10 @@
         for j in range(3):
             total = total + decode(zrb.at[j, i])
         total = jnp.where(mine + i < table_ref[192], total.T, jnp.zeros((BLK, BLK), F32))
-        bgv[mine + i] = total.astype(BF16)
+        bg_ref[mine + i] = total.astype(BF16)
 
     def slots(dx, dzh, n=2, half=c):
-        return bgv.at[pl.ds(half * 32 + lax.rem(x + dx + NX, NX) * 8 + lax.rem(zh + dzh + NZH, NZH) * 2, n)]
+        return bg_ref.at[pl.ds(half * 32 + lax.rem(x + dx + NX, NX) * 8 + lax.rem(zh + dzh + NZH, NZH) * 2, n)]
 
     def put(part, ss, rs, dev):
         copy = remote(part, part, ss, rs, dev)
@@ -350,10 +350,6 @@
         part = slots(2, -k)
         remote(part, part, gfs.at[k], gfr.at[k], core).wait_recv()
         over(3, k)
-
-    def write(half, m):
-        part = pl.ds(half * 32 + lax.rem(x + (0, -1, 1, 2)[m] + NX, NX) * 8, 8)
-        return pltpu.make_async_copy(bgv.at[part], bg_ref.at[part], os.at[(0 if half is c else 4) + m])
 
     for k in (2, 1, 3):
         put(slots(0, 0), gzs.at[k], gzr.at[k], zhs[k])
@@ -369,7 +365,6 @@
         over(0, k)
         if k == 1:
             gx_pass(0)
-    write(c, 0).start()
 
     def z_copy(j):
         return remote(dxb.at[1 - zl, 0, j], dxz.at[j], dzs.at[j], dzr.at[j], zp)
@@ -387,64 +382,53 @@
     y_part(-2, 1)
     y_part(2, 1)
     gx_pass(2)
-    write(c, 1).start()
-    write(c, 2).start()
     y_part(-3, 1)
     y_part(3, 1)
     y_part(-4, 1)
-    youtv[...] = yacc[...].astype(BF16)
-    ywrite = pltpu.make_async_copy(youtv, y_ref, os.at[8])
-    ywrite.start()
+    y_ref[...] = yacc[...].astype(BF16)
     for j in range(SUB):
         part = dxz.at[j]
         remote(part, part, dzs.at[j], dzr.at[j], core).wait_recv()
-        dxv[:, j * BLK : (j + 1) * BLK] = (dxf[zl, j] + decode(part)).astype(BF16)
-    dxwrite = pltpu.make_async_copy(dxv, dx_ref, os.at[9])
-    dxwrite.start()
+        dx_ref[:, j * BLK : (j + 1) * BLK] = (dxf[zl, j] + decode(part)).astype(BF16)
+    for j in range(3):
+        wz_copy(j).wait_send()
+
+    for way in (0, 1):
+
+        def left(n, carry, way=way):
+            dx_copy(way, lax.div(n, SUB), lax.rem(n, SUB)).wait_send()
+            return carry
+
+        lax.fori_loop(SUB, 7 * SUB, left, 0)
+    for o in range(3):
+
+        def gone(j, carry, o=o):
+            dw_copy(o, j).wait_send()
+            return carry
+
+        lax.fori_loop(0, 4, gone, 0)
+
     for k in (0, 1, 3, 2):
         gf_take(k)
-    write(c, 3).start()
     for m in range(4):
         for k in range(4):
             part = slots((0, -1, 1, 2)[m], -k, 2, 1 - c)
             remote(part, part, gcs.at[m, k], gcr.at[m, k], core).wait_recv()
-        write(1 - c, m).start()
 
     for copy in sent[from_gather:]:
         copy.wait_send()
     for j in range(SUB):
         z_copy(j).wait_send()
-    for j in range(3):
-        wz_copy(j).wait_send()
-
-    for way in (0, 1):
-
-        def left(n, carry, way=way):
-            dx_copy(way, lax.div(n, SUB), lax.rem(n, SUB)).wait_send()
-            return carry
-
-        lax.fori_loop(SUB, 7 * SUB, left, 0)
-    for o in range(3):
-
-        def gone(j, carry, o=o):
-            dw_copy(o, j).wait_send()
-            return carry
-
-        lax.fori_loop(0, 4, gone, 0)
-    for m in range(4):
-        write(c, m).wait()
-        write(1 - c, m).wait()
-    ywrite.wait()
-    dxwrite.wait()
 
 
 def per_device(tokens, cotangent, blocks, slot_block, shard_count):
-    cell = slot_block // 32 * 2 + slot_block % 2
-    place = jnp.arange(64, dtype=jnp.int32)
-    here = (cell[:, None] == jnp.arange(128, dtype=jnp.int32)[None, :]) & (place < shard_count[0])[:, None]
-    cell_slot = jnp.max(jnp.where(here, place[:, None], -1), axis=0)
-    table = jnp.concatenate([cell_slot, slot_block, shard_count])
-    smem, hbm = pl.BlockSpec(memory_space=pltpu.SMEM), pl.BlockSpec(memory_space=pltpu.HBM)
+    n = jnp.arange(193, dtype=jnp.int32)[:, None]
+    place = jnp.arange(64, dtype=jnp.int32)[None, :]
+    block = n // 2 * 32 + lax.axis_index("fsdp") * 2 + n % 2
+    held = (slot_block[None, :] == block) & (place < shard_count[0])
+    entry = jnp.where(n < 128, jnp.where(held, place, -1), jnp.where(place == n - 128, slot_block[None, :], -1))
+    table = jnp.max(jnp.where(n < 192, entry, shard_count[0]), axis=1)
+    smem, vmem, hbm = (pl.BlockSpec(memory_space=m) for m in (pltpu.SMEM, pltpu.VMEM, pltpu.HBM))
     dma = pltpu.SemaphoreType.DMA
     return pl.pallas_call(
         kernel,
@@ -454,7 +438,7 @@
             jax.ShapeDtypeStruct((64, BLK, BLK), BF16),
         ),
         in_specs=[smem] + [hbm] * 3,
-        out_specs=(hbm,) * 3,
+        out_specs=(vmem,) * 3,
         scratch_shapes=[
             pltpu.VMEM((64, 2 * TOK, BLK), BF16),
             pltpu.VMEM((2 * TOK, CF), BF16),
@@ -471,13 +455,10 @@
             pltpu.VMEM((2, BLK, BLK), F32),
             pltpu.VMEM((3, 2, CODE, BLK), jnp.int32),
             pltpu.VMEM((3, 2, CODE, BLK), jnp.int32),
-            pltpu.VMEM((64, BLK, BLK), BF16),
-            pltpu.VMEM((TOK, CF), BF16),
-            pltpu.VMEM((TOK, XF), BF16),
             dma((6,)), dma((40,)), dma((40,)), dma((17,)), dma((17,)),
             dma((2, 8, SUB)), dma((2, 8, SUB)), dma((SUB,)), dma((SUB,)),
             dma((3, 4)), dma((3, 4)), dma((3,)), dma((3,)),
-            dma((4,)), dma((4,)), dma((2, 4)), dma((2, 4)), dma((4,)), dma((4,)), dma((4, 4)), dma((4, 4)), dma((10,)),
+            dma((4,)), dma((4,)), dma((2, 4)), dma((2, 4)), dma((4,)), dma((4,)), dma((4, 4)), dma((4, 4)),
         ],
         compiler_params=pltpu.CompilerParams(
             collective_id=0, has_side_effects=True, vmem_limit_bytes=50 << 20

time: 84.7 us -> 83.5 us (0.986)
  no operation moved by 1% of the time
where the time goes in v4:
time: 83.5 us; the launch traced here: 83.2 us
  Pallas kernels  76.8 us (92%)
  local copies, waits for them, and re-layouts  4.34 us (5%)
  between operations  1.32 us (2%)
    pallas_call x1, Pallas kernels, per_device(): pl.pallas_call(kernel, out_shape=(jax.ShapeDtypeStruct((TOK, CF), BF16),...  76.8 us
    unnamed x7, local copies, waits for them, and re-layouts  4.34 us

profile of v4, /device:TPU:1, one launch (start us, length us, event | category | flops | bytes accessed | tf_op | source)
XLA Modules:
  0.0 83.2 jit_solution(15122063312917944318)
XLA Ops:
  1.3 0.8 select_reduce_fusion.table_ref
  2.1 0.0 copy-start
  2.1 0.9 %copy-done = bf16[128,512]{1,0:T(8,128)(2,1)S(1)} copy-done((bf16[128,512]{1,0:T(8,128)(2,1)S(1)}, bf16[128,512]{1,0:T(8,128)(2,1)}, u32[]{:S(2)}) %copy-start) | copy-done | bytes 131096
  3.0 0.0 copy-start.1
  3.0 0.8 %copy-done.1 = bf16[128,256]{1,0:T(8,128)(2,1)S(1)} copy-done((bf16[128,256]{1,0:T(8,128)(2,1)S(1)}, bf16[128,256]{1,0:T(8,128)(2,1)}, u32[]{:S(2)}) %copy-start.1) | copy-done | bytes 65560
  3.8 76.8 %shard_map.76 = (bf16[128,256]{1,0:T(8,128)(2,1)S(1)}, bf16[128,512]{1,0:T(8,128)(2,1)S(1)}, bf16[64,128,128]{2,1,0:T(8,128)(2,1)S(1)}) custom-call(s32[193]{0:T(256)S(1)} %select_reduce_fusion.table_ref, bf16[128,512]{1,0:T(8,128)(2,1)S(1)} %copy-done, bf16[128,256]{1,0:T(8,128)(2,1)S(1)} %copy-done.1, bf16[64,128,128]{2,1,0:T(8,128)(2,1)} %blk_hbm.1), custom_call_target="tpu_custom_call" | custom-call | tf_op jit(solution)/shard_map/pallas_call | solution.py:433
  80.6 0.6 copy.12
  81.3 0.7 copy.13
  81.9 1.3 %copy.14 = bf16[64,128,128]{2,1,0:T(8,128)(2,1)} copy(bf16[64,128,128]{2,1,0:T(8,128)(2,1)S(1)} %get-tuple-element.12) | data formatting | bytes 4194304
  (3 shorter events, 0.0 us)
Async XLA Ops:
  2.1 0.9 %copy-start = (bf16[128,512]{1,0:T(8,128)(2,1)S(1)}, bf16[128,512]{1,0:T(8,128)(2,1)}, u32[]{:S(2)}) copy-start(bf16[128,512]{1,0:T(8,128)(2,1)} %tok_hbm.1) | copy-start | bytes 393220
  3.0 0.8 %copy-start.1 = (bf16[128,256]{1,0:T(8,128)(2,1)S(1)}, bf16[128,256]{1,0:T(8,128)(2,1)}, u32[]{:S(2)}) copy-start(bf16[128,256]{1,0:T(8,128)(2,1)} %ct_hbm.1) | copy-start | bytes 196612

commit v5 on v4

--- a/solution.py
+++ b/solution.py
@@ -297,8 +297,9 @@
         if j < 3:
             wz_copy(j).start()
 
-    lax.fori_loop(0, 4, dw_send, 0)
+    lax.fori_loop(0, 2, dw_send, 0)
     dx_round(2)
+    lax.fori_loop(2, 4, dw_send, 0)
     y_part(-3, 0)
     dw_sum(0)
     dx_round(3)

time: 83.5 us -> 83.5 us (level)
  no operation moved by 1% of the time
where the time goes in v5:
time: 83.5 us; the launch traced here: 83.2 us
  Pallas kernels  76.8 us (92%)
  local copies, waits for them, and re-layouts  4.34 us (5%)
  between operations  1.32 us (2%)
    pallas_call x1, Pallas kernels, per_device(): pl.pallas_call(kernel, out_shape=(jax.ShapeDtypeStruct((TOK, CF), BF16),...  76.8 us
    unnamed x7, local copies, waits for them, and re-layouts  4.34 us

profile of v5, /device:TPU:1, one launch (start us, length us, event | category | flops | bytes accessed | tf_op | source)
XLA Modules:
  0.0 83.2 jit_solution(18201571422896372257)
XLA Ops:
  1.3 0.8 select_reduce_fusion.table_ref
  2.1 0.0 copy-start
  2.1 0.9 %copy-done = bf16[128,512]{1,0:T(8,128)(2,1)S(1)} copy-done((bf16[128,512]{1,0:T(8,128)(2,1)S(1)}, bf16[128,512]{1,0:T(8,128)(2,1)}, u32[]{:S(2)}) %copy-start) | copy-done | bytes 131096
  3.0 0.0 copy-start.1
  3.0 0.8 %copy-done.1 = bf16[128,256]{1,0:T(8,128)(2,1)S(1)} copy-done((bf16[128,256]{1,0:T(8,128)(2,1)S(1)}, bf16[128,256]{1,0:T(8,128)(2,1)}, u32[]{:S(2)}) %copy-start.1) | copy-done | bytes 65560
  3.8 76.8 %shard_map.76 = (bf16[128,256]{1,0:T(8,128)(2,1)S(1)}, bf16[128,512]{1,0:T(8,128)(2,1)S(1)}, bf16[64,128,128]{2,1,0:T(8,128)(2,1)S(1)}) custom-call(s32[193]{0:T(256)S(1)} %select_reduce_fusion.table_ref, bf16[128,512]{1,0:T(8,128)(2,1)S(1)} %copy-done, bf16[128,256]{1,0:T(8,128)(2,1)S(1)} %copy-done.1, bf16[64,128,128]{2,1,0:T(8,128)(2,1)} %blk_hbm.1), custom_call_target="tpu_custom_call" | custom-call | tf_op jit(solution)/shard_map/pallas_call | solution.py:434
  80.6 0.6 copy.12
  81.3 0.7 copy.13
  81.9 1.3 %copy.14 = bf16[64,128,128]{2,1,0:T(8,128)(2,1)} copy(bf16[64,128,128]{2,1,0:T(8,128)(2,1)S(1)} %get-tuple-element.12) | data formatting | bytes 4194304
  (3 shorter events, 0.0 us)
Async XLA Ops:
  2.1 0.9 %copy-start = (bf16[128,512]{1,0:T(8,128)(2,1)S(1)}, bf16[128,512]{1,0:T(8,128)(2,1)}, u32[]{:S(2)}) copy-start(bf16[128,512]{1,0:T(8,128)(2,1)} %tok_hbm.1) | copy-start | bytes 393220
  3.0 0.8 %copy-start.1 = (bf16[128,256]{1,0:T(8,128)(2,1)S(1)}, bf16[128,256]{1,0:T(8,128)(2,1)}, u32[]{:S(2)}) copy-start(bf16[128,256]{1,0:T(8,128)(2,1)} %ct_hbm.1) | copy-start | bytes 196612
